TPU v7x, 32 devices: a whole 2x2x4 slice. The times are simulated.
32 devices in a mesh: grp: 4 (over y, x), dom: 8 (over z, core).
Axes of the slice: x: 2, y: 2, z: 4, core: 2. Of those that a mesh axis runs over, the one named last changes fastest.
Arguments:
- node_in: bfloat16 [131072, 128], P(('grp', 'dom')), may hold values from -6 to 6
- edge_in: bfloat16 [1048576, 128], P(('grp', 'dom')), may hold values from -6 to 6
- edge_slot: int32 [1048576], P(('grp', 'dom')), may hold values from 0 to 2047, as said below
- edge_receiver: int32 [1048576], P(('grp', 'dom')), may hold values from 0 to 4095, as said below
- edge_count: int32 [32], P(('grp', 'dom')), may hold values from 10922 to 32768
- request: int32 [32, 8, 256], P(('grp', 'dom')), may hold values from 0 to 4095, as said below
- node_cot: bfloat16 [131072, 128], P(('grp', 'dom')), may hold values from -6 to 6
- edge_cot: bfloat16 [1048576, 128], P(('grp', 'dom')), may hold values from -6 to 6
- edge_entry: float32 [384, 128], replicated, may hold values from -0.3125 to 0.3125
- edge_entry_mean: float32 [384, 128], replicated, may hold values from -0.015625 to 0.015625
- edge_entry_var: float32 [384, 128], replicated, may hold values from 2.2e-06 to 3.6e-05
- edge_entry_ema: float32 [384, 128], replicated, may hold values from -0.3125 to 0.3125
- node_entry: float32 [256, 128], replicated, may hold values from -0.375 to 0.375
- node_entry_mean: float32 [256, 128], replicated, may hold values from -0.015625 to 0.015625
- node_entry_var: float32 [256, 128], replicated, may hold values from 2.2e-06 to 3.6e-05
- node_entry_ema: float32 [256, 128], replicated, may hold values from -0.375 to 0.375
- inner_layers: float32 [4, 128, 128], replicated, may hold values from -0.5 to 0.5
- inner_layers_mean: float32 [4, 128, 128], replicated, may hold values from -0.015625 to 0.015625
- inner_layers_var: float32 [4, 128, 128], replicated, may hold values from 2.2e-06 to 3.6e-05
- inner_layers_ema: float32 [4, 128, 128], replicated, may hold values from -0.5 to 0.5
- vectors: float32 [10, 128], replicated
- vectors_mean: float32 [10, 128], replicated, may hold values from -0.015625 to 0.015625
- vectors_var: float32 [10, 128], replicated, may hold values from 2.2e-06 to 3.6e-05
- vectors_ema: float32 [10, 128], replicated
Outputs:
- node_out: bfloat16 [131072, 128], P(('grp', 'dom'))
- edge_out: bfloat16 [1048576, 128], P(('grp', 'dom'))
- node_grad: float32 [131072, 128], P(('grp', 'dom'))
- edge_grad: float32 [1048576, 128], P(('grp', 'dom'))
- grad_norm: float32 [], replicated
- edge_entry_mean_new: float32 [384, 128], replicated
- edge_entry_var_new: float32 [384, 128], replicated
- edge_entry_new: float32 [384, 128], replicated
- edge_entry_copy: bfloat16 [384, 128], replicated
- edge_entry_ema_new: float32 [384, 128], replicated
- node_entry_mean_new: float32 [256, 128], replicated
- node_entry_var_new: float32 [256, 128], replicated
- node_entry_new: float32 [256, 128], replicated
- node_entry_copy: bfloat16 [256, 128], replicated
- node_entry_ema_new: float32 [256, 128], replicated
- inner_layers_mean_new: float32 [4, 128, 128], replicated
- inner_layers_var_new: float32 [4, 128, 128], replicated
- inner_layers_new: float32 [4, 128, 128], replicated
- inner_layers_copy: bfloat16 [4, 128, 128], replicated
- inner_layers_ema_new: float32 [4, 128, 128], replicated
- vectors_mean_new: float32 [10, 128], replicated
- vectors_var_new: float32 [10, 128], replicated
- vectors_new: float32 [10, 128], replicated
- vectors_copy: bfloat16 [10, 128], replicated
- vectors_ema_new: float32 [10, 128], replicated
Inputs may be any that keep to these rules, and one draw needn't show every extreme that they name: `edge_slot`: slot q * 256 + s names request[r, q, s] of the edge's device r; the rows of local edge block k (local rows 128 * k to 128 * k + 127, padding included) read slots k * 8 to (k + 1) * 8 - 1 only. `edge_receiver`: the rows of local edge block k (padding included) receive at local particles k * 16 to (k + 1) * 16 - 1 only. `request`: the 256 particles that a device requests from one device are distinct.
All inputs are finite; a program needn't handle non-finite values.
Results may differ from a plain program's by a relative error of at most 0.011.
Values may be sent and summed in bfloat16 or wider, within the bound.
A program may use at most 320 MiB of HBM per device.

v0:
```python
import math

import jax
import jax.numpy as jnp
from jax import lax
from jax.sharding import PartitionSpec as P

STEP = 10


eps_norm = 1e-05
beta_one = 0.5
beta_two = 0.6
learn_rate = 0.08
decay_rate = 0.01
adam_eps = 1e-08
ema_keep = 0.9
clip_level = 1.0


def matmul(operand, weights):
    return jnp.dot(operand, weights, preferred_element_type=jnp.float32)


def matmul_nt(operand, weights):
    return lax.dot_general(
        operand, weights, (((1,), (1,)), ((), ())), preferred_element_type=jnp.float32
    )


def matmul_tn(operand, weights):
    return lax.dot_general(
        operand, weights, (((0,), (0,)), ((), ())), preferred_element_type=jnp.float32
    )


def layer_norm(values):
    center = values - jnp.mean(values, axis=1, keepdims=True)
    inverse = lax.rsqrt(jnp.mean(center * center, axis=1, keepdims=True) + eps_norm)
    return (center * inverse, inverse)


def norm_back(upper, normed, inverse):
    mean_plain = jnp.mean(upper, axis=1, keepdims=True)
    mean_cross = jnp.mean(upper * normed, axis=1, keepdims=True)
    return inverse * (upper - mean_plain - normed * mean_cross)


def gelu_back(before, upper):
    return jax.vjp(jax.nn.gelu, before)[1](upper)[0]


def column_sum(values):
    return jnp.sum(values.astype(jnp.float32), axis=0)


def window_onehot(index, width, dtype):
    blocks = index.shape[0] // 128
    local_ids = index.reshape(blocks, 128) - (jnp.arange(blocks, dtype=jnp.int32) * width)[:, None]
    return (local_ids[:, :, None] == jnp.arange(width, dtype=jnp.int32)[None, None, :]).astype(
        dtype
    )


def window_take(onehot, table):
    blocks, rows_in, width = onehot.shape
    shaped = table.reshape(blocks, width, table.shape[1])
    if table.dtype == jnp.float32:
        picked = jnp.einsum(
            "bew,bwl->bel",
            onehot,
            shaped,
            precision=lax.Precision.HIGHEST,
            preferred_element_type=jnp.float32,
        )
    else:
        picked = jnp.einsum("bew,bwl->bel", onehot, shaped, preferred_element_type=jnp.float32)
    return picked.reshape(blocks * rows_in, table.shape[1]).astype(table.dtype)


def window_add(onehot, values):
    blocks, rows_in, width = onehot.shape
    shaped = values.reshape(blocks, rows_in, values.shape[1])
    total = jnp.einsum(
        "bew,bel->bwl",
        onehot,
        shaped,
        precision=lax.Precision.HIGHEST,
        preferred_element_type=jnp.float32,
    )
    return total.reshape(blocks * width, values.shape[1])


def pick_rows(table, index):
    count = index.shape[0]
    step = math.gcd(count, 2048)
    columns = jnp.arange(table.shape[0], dtype=jnp.int32)

    def pick_one_block(ids):
        onehot = (ids[:, None] == columns[None, :]).astype(table.dtype)
        return matmul(onehot, table).astype(table.dtype)

    return lax.map(pick_one_block, index.reshape(count // step, step)).reshape(
        count, table.shape[1]
    )


def add_rows(values, index, count):
    total_rows = index.shape[0]
    step = math.gcd(total_rows, 2048)
    columns = jnp.arange(count, dtype=jnp.int32)

    def add_one_block(carry, item):
        ids, rows = item
        onehot = (ids[:, None] == columns[None, :]).astype(rows.dtype)
        return (carry + matmul_tn(onehot, rows), None)

    start = jnp.zeros((count, values.shape[1]), jnp.float32)
    items = (
        index.reshape(total_rows // step, step),
        values.reshape(total_rows // step, step, values.shape[1]),
    )
    return lax.scan(add_one_block, start, items)[0]


def adamw_step(master, moment_mean, moment_var, average, gradient, factor):
    clipped = gradient * factor
    mean_new = beta_one * moment_mean + (1.0 - beta_one) * clipped
    var_new = beta_two * moment_var + (1.0 - beta_two) * clipped * clipped
    mean_hat = mean_new / (1.0 - beta_one**STEP)
    var_hat = var_new / (1.0 - beta_two**STEP)
    updated = master - learn_rate * (
        mean_hat / (jnp.sqrt(var_hat) + adam_eps) + decay_rate * master
    )
    return (
        mean_new,
        var_new,
        updated,
        updated.astype(jnp.bfloat16),
        ema_keep * average + (1.0 - ema_keep) * updated,
    )


def shards(
    node_in,
    edge_in,
    edge_slot,
    edge_receiver,
    edge_count,
    request,
    node_cot,
    edge_cot,
    edge_entry,
    edge_entry_mean,
    edge_entry_var,
    edge_entry_ema,
    node_entry,
    node_entry_mean,
    node_entry_var,
    node_entry_ema,
    inner_layers,
    inner_layers_mean,
    inner_layers_var,
    inner_layers_ema,
    vectors,
    vectors_mean,
    vectors_var,
    vectors_ema,
):
    rows_count = node_in.shape[0]
    width = node_in.shape[1]
    peers = lax.axis_size("dom")
    slots = request.shape[2]
    edge_blocks = edge_in.shape[0] // 128
    receive_window = rows_count // edge_blocks
    slot_window = peers * slots // edge_blocks
    edge_low = edge_entry.astype(jnp.bfloat16)
    node_low = node_entry.astype(jnp.bfloat16)
    inner_low = inner_layers.astype(jnp.bfloat16)
    wanted = request[0]
    asked = lax.all_to_all(wanted, "dom", split_axis=0, concat_axis=0, tiled=True)
    outgoing = pick_rows(node_in, asked.reshape(-1)).reshape(peers, slots, width)
    slot_rows = lax.all_to_all(outgoing, "dom", split_axis=0, concat_axis=0, tiled=True).reshape(
        peers * slots, width
    )
    slot_hot = window_onehot(edge_slot, slot_window, jnp.bfloat16)
    slot_hot_wide = window_onehot(edge_slot, slot_window, jnp.float32)
    receive_hot = window_onehot(edge_receiver, receive_window, jnp.bfloat16)
    receive_hot_wide = window_onehot(edge_receiver, receive_window, jnp.float32)
    sender_rows = window_take(slot_hot, slot_rows)
    receiver_rows = window_take(receive_hot, node_in)
    live = (jnp.arange(edge_in.shape[0], dtype=jnp.int32) < edge_count[0]).astype(jnp.float32)[
        :, None
    ]
    pre_one = (
        matmul(edge_in, edge_low[:width])
        + matmul(sender_rows, edge_low[width : 2 * width])
        + matmul(receiver_rows, edge_low[2 * width :])
        + vectors[0]
    )
    act_one = jax.nn.gelu(pre_one).astype(jnp.bfloat16)
    pre_two = matmul(act_one, inner_low[0]) + vectors[1]
    act_two = jax.nn.gelu(pre_two).astype(jnp.bfloat16)
    pre_three = matmul(act_two, inner_low[1]) + vectors[2]
    edge_normed, edge_inverse = layer_norm(pre_three)
    message = live * (edge_normed * vectors[3] + vectors[4])
    edge_out = (edge_in.astype(jnp.float32) + message).astype(jnp.bfloat16)
    gathered = window_add(receive_hot_wide, message).astype(jnp.bfloat16)
    node_one = matmul(node_in, node_low[:width]) + matmul(gathered, node_low[width:]) + vectors[5]
    node_act_one = jax.nn.gelu(node_one).astype(jnp.bfloat16)
    node_two = matmul(node_act_one, inner_low[2]) + vectors[6]
    node_act_two = jax.nn.gelu(node_two).astype(jnp.bfloat16)
    node_three = matmul(node_act_two, inner_low[3]) + vectors[7]
    node_normed, node_inverse = layer_norm(node_three)
    node_out = (node_in.astype(jnp.float32) + node_normed * vectors[8] + vectors[9]).astype(
        jnp.bfloat16
    )
    upstream = node_cot.astype(jnp.float32)
    edge_upstream = edge_cot.astype(jnp.float32)
    grad_node_gain = jnp.sum(upstream * node_normed, axis=0)
    grad_node_shift = jnp.sum(upstream, axis=0)
    node_d_three = norm_back(upstream * vectors[8], node_normed, node_inverse).astype(jnp.bfloat16)
    grad_node_inner_two = matmul_tn(node_act_two, node_d_three)
    node_d_two = gelu_back(node_two, matmul_nt(node_d_three, inner_low[3])).astype(jnp.bfloat16)
    grad_node_inner_one = matmul_tn(node_act_one, node_d_two)
    node_d_one = gelu_back(node_one, matmul_nt(node_d_two, inner_low[2])).astype(jnp.bfloat16)
    grad_node_entry = jnp.concatenate(
        [matmul_tn(node_in, node_d_one), matmul_tn(gathered, node_d_one)], axis=0
    )
    node_input_grad = matmul_nt(node_d_one, node_low)
    node_grad = upstream + node_input_grad[:, :width]
    message_grad = live * (
        window_take(receive_hot_wide, node_input_grad[:, width:]) + edge_upstream
    )
    grad_edge_gain = jnp.sum(message_grad * edge_normed, axis=0)
    grad_edge_shift = jnp.sum(message_grad, axis=0)
    edge_d_three = norm_back(message_grad * vectors[3], edge_normed, edge_inverse).astype(
        jnp.bfloat16
    )
    grad_edge_inner_two = matmul_tn(act_two, edge_d_three)
    edge_d_two = gelu_back(pre_two, matmul_nt(edge_d_three, inner_low[1])).astype(jnp.bfloat16)
    grad_edge_inner_one = matmul_tn(act_one, edge_d_two)
    edge_d_one = gelu_back(pre_one, matmul_nt(edge_d_two, inner_low[0])).astype(jnp.bfloat16)
    grad_edge_entry = jnp.concatenate(
        [
            matmul_tn(edge_in, edge_d_one),
            matmul_tn(sender_rows, edge_d_one),
            matmul_tn(receiver_rows, edge_d_one),
        ],
        axis=0,
    )
    edge_input_grad = matmul_nt(edge_d_one, edge_low)
    edge_grad = edge_upstream + edge_input_grad[:, :width]
    node_grad = node_grad + window_add(receive_hot_wide, edge_input_grad[:, 2 * width :])
    slot_grad = window_add(slot_hot_wide, edge_input_grad[:, width : 2 * width]).astype(
        jnp.bfloat16
    )
    returned = lax.all_to_all(
        slot_grad.reshape(peers, slots, width), "dom", split_axis=0, concat_axis=0, tiled=True
    )
    node_grad = node_grad + add_rows(
        returned.reshape(peers * slots, width), asked.reshape(-1), rows_count
    )
    grad_inner = jnp.stack(
        [grad_edge_inner_one, grad_edge_inner_two, grad_node_inner_one, grad_node_inner_two]
    )
    grad_vectors = jnp.stack(
        [
            column_sum(edge_d_one),
            column_sum(edge_d_two),
            column_sum(edge_d_three),
            grad_edge_gain,
            grad_edge_shift,
            column_sum(node_d_one),
            column_sum(node_d_two),
            column_sum(node_d_three),
            grad_node_gain,
            grad_node_shift,
        ]
    )
    summed = lax.psum((grad_edge_entry, grad_node_entry, grad_inner, grad_vectors), ("grp", "dom"))
    total = (
        jnp.sum(summed[0] * summed[0])
        + jnp.sum(summed[1] * summed[1])
        + jnp.sum(summed[2] * summed[2])
        + jnp.sum(summed[3] * summed[3])
    )
    grad_norm = jnp.sqrt(total)
    factor = clip_level / jnp.maximum(grad_norm, clip_level)
    first_set = adamw_step(
        edge_entry, edge_entry_mean, edge_entry_var, edge_entry_ema, summed[0], factor
    )
    second_set = adamw_step(
        node_entry, node_entry_mean, node_entry_var, node_entry_ema, summed[1], factor
    )
    third_set = adamw_step(
        inner_layers, inner_layers_mean, inner_layers_var, inner_layers_ema, summed[2], factor
    )
    fourth_set = adamw_step(vectors, vectors_mean, vectors_var, vectors_ema, summed[3], factor)
    return (
        node_out,
        edge_out,
        node_grad,
        edge_grad,
        grad_norm,
        first_set[0],
        first_set[1],
        first_set[2],
        first_set[3],
        first_set[4],
        second_set[0],
        second_set[1],
        second_set[2],
        second_set[3],
        second_set[4],
        third_set[0],
        third_set[1],
        third_set[2],
        third_set[3],
        third_set[4],
        fourth_set[0],
        fourth_set[1],
        fourth_set[2],
        fourth_set[3],
        fourth_set[4],
    )


def solution(mesh):
    in_specs = (
        P(("grp", "dom"), None),
        P(("grp", "dom"), None),
        P(("grp", "dom")),
        P(("grp", "dom")),
        P(("grp", "dom")),
        P(("grp", "dom"), None, None),
        P(("grp", "dom"), None),
        P(("grp", "dom"), None),
        P(),
        P(),
        P(),
        P(),
        P(),
        P(),
        P(),
        P(),
        P(),
        P(),
        P(),
        P(),
        P(),
        P(),
        P(),
        P(),
    )
    out_specs = (
        P(("grp", "dom"), None),
        P(("grp", "dom"), None),
        P(("grp", "dom"), None),
        P(("grp", "dom"), None),
        P(),
        P(),
        P(),
        P(),
        P(),
        P(),
        P(),
        P(),
        P(),
        P(),
        P(),
        P(),
        P(),
        P(),
        P(),
        P(),
        P(),
        P(),
        P(),
        P(),
        P(),
    )
    return jax.shard_map(shards, mesh=mesh, in_specs=in_specs, out_specs=out_specs, check_vma=False)
```

profile of v0, /device:TPU:0, one launch (start us, length us, event | category | flops | bytes accessed | tf_op | source)
XLA Modules:
  0.0 575.1 jit_solution(14943148945292094751)
XLA Ops:
  8.5 6.3 %all-to-all-start = ((s32[8,1,256]{2,1,0:T(1,128)}), s32[8,1,256]{2,1,0:T(1,128)S(1)}, u32[]{:S(2)}, u32[]{:S(2)}) async-start(s32[8,1,256]{2,1,0:T(1,128)} %all_to_all.12), calls=%async_computation | async-start | bytes 16384 | tf_op jit(solution)/shard_map/all_to_all | solution.py:181
  18.8 3.0 fusion.65
  21.9 12.0 %fusion.63 = f32[32768,128]{1,0:T(8,128)} fusion(bf16[32768,128]{1,0:T(8,128)(2,1)} %param.25, bf16[384,128]{1,0:T(8,128)(2,1)S(1)} %convert_element_type.134), kind=kOutput, calls=%fused_computation.149 | convolution fusion | flops 1073741824 | bytes 25198592 | tf_op jit(solution)/shard_map/dot_general | solution.py:22
  37.8 6.7 %fusion.25 = bf16[2048,128]{1,0:T(8,128)(2,1)} fusion(bf16[4096,128]{1,0:T(8,128)(2,1)S(1)} %copy-done.2, s32[2048]{0:T(1024)S(1)} %bitcast.159), kind=kOutput, calls=%fused_computation.62 | convolution fusion | flops 2156134400 | bytes 1581056 | tf_op jit(solution)/shard_map/while/body/eval_jaxpr/dot_general | solution.py:22
  44.4 5.6 all-to-all-start.1
  50.7 6.7 %convolution_convert_fusion = bf16[256,128,128]{2,1,0:T(8,128)(2,1)} fusion(bf16[256,16,128]{2,1,0:T(8,128)(2,1)S(1)} %bitcast.154, s32[256,128]{1,0:T(8,128)S(1)} %bitcast_subtract_fusion.1), kind=kOutput, calls=%fused_computation.44 | convolution fusion | flops 138936320 | bytes 9568256 | tf_op jit(solution)/shard_map/bew,bwl->bel/dot_general | solution.py:77
  57.4 8.0 %all-to-all-done.1 = bf16[8,256,128]{2,1,0:T(8,128)(2,1)S(1)} async-done(((bf16[8,256,128]{2,1,0:T(8,128)(2,1)}), bf16[8,256,128]{2,1,0:T(8,128)(2,1)S(1)}, u32[]{:S(2)}, u32[]{:S(2)}) %all-to-all-start.1) | async-done | bytes 524320 | tf_op jit(solution)/shard_map/all_to_all | solution.py:183
  65.3 6.7 %convolution_convert_fusion.1 = bf16[256,128,128]{2,1,0:T(8,128)(2,1)} fusion(bf16[256,8,128]{2,1,0:T(8,128)(2,1)S(1)} %bitcast.158, s32[256,128]{1,0:T(8,128)S(1)} %bitcast_subtract_fusion), kind=kOutput, calls=%fused_computation.45 | convolution fusion | flops 71565312 | bytes 9043968 | tf_op jit(solution)/shard_map/bew,bwl->bel/dot_general | solution.py:77
  72.0 16.8 %convolution_add_fusion.3 = f32[32768,128]{1,0:T(8,128)} fusion(f32[32768,128]{1,0:T(8,128)} %fusion.63, bf16[32768,128]{1,0:T(8,128)(2,1)} %bitcast.144, bf16[384,128]{1,0:T(8,128)(2,1)S(1)} %convert_element_type.134), kind=kOutput, calls=%fused_computation.4 | convolution fusion | flops 1077936128 | bytes 41975808 | tf_op jit(solution)/shard_map/dot_general | solution.py:22
  88.9 10.8 %fusion = f32[32768,128]{1,0:T(8,128)} fusion(f32[32768,128]{1,0:T(8,128)} %convolution_add_fusion.3, bf16[32768,128]{1,0:T(8,128)(2,1)S(1)} %bitcast.140, f32[128]{0:T(128)S(1)} %get-tuple-element.178, bf16[384,128]{1,0:T(8,128)(2,1)S(1)} %convert_element_type.134), kind=kOutput, calls=%fused_computation.3 | convolution fusion | flops 1082130432 | bytes 41976320 | tf_op jit(solution)/shard_map/dot_general | solution.py:22
  99.6 12.7 %convolution_add_fusion.1 = f32[32768,128]{1,0:T(8,128)} fusion(f32[128]{0:T(128)S(1)} %get-tuple-element.177, bf16[4,128,128]{2,1,0:T(8,128)(2,1)S(1)} %convert_element_type.141, f32[32768,128]{1,0:T(8,128)} %fusion), kind=kOutput, calls=%fused_computation.1 | convolution fusion | flops 1115684864 | bytes 33587712 | tf_op jit(solution)/shard_map/dot_general | solution.py:22
  112.4 13.8 %fusion.79 = (f32[32768]{0:T(1024)S(1)}, f32[32768,128]{1,0:T(8,128)}) fusion(f32[128]{0:T(128)} %get-tuple-element.176, bf16[4,128,128]{2,1,0:T(8,128)(2,1)S(1)} %convert_element_type.141, f32[32768,128]{1,0:T(8,128)} %convolution_add_fusion.1), kind=kOutput, calls=%fused_computation.181 | convolution fusion | flops 1119846400 | bytes 33718784 | tf_op jit(solution)/shard_map/dot_general | solution.py:22
  126.2 11.5 %multiply_reduce_fusion.2 = f32[32768]{0:T(1024)S(1)} fusion(f32[32768,128]{1,0:T(8,128)} %get-tuple-element.181, f32[32768]{0:T(1024)S(1)} %broadcast_multiply_fusion.5), kind=kLoop, calls=%fused_computation.37 | loop fusion | flops 12550144 | bytes 17039360 | tf_op jit(solution)/shard_map/reduce_sum | solution.py:39
  137.8 16.7 %add_convert_fusion = (bf16[32768,128]{1,0:T(8,128)(2,1)}, f32[32768,128]{1,0:T(8,128)}) fusion(bf16[32768,128]{1,0:T(8,128)(2,1)S(1)} %bitcast.147, f32[128]{0:T(128)S(1)} %copy-done.43, f32[128]{0:T(128)S(1)} %get-tuple-element.175, f32[32768]{0:T(1024)S(1)} %add_rsqrt_fusion, f32[32768,128]{1,0:T(8,128)S(1)} %copy-done, ...), kind=kLoop, calls=%fused_computation.35 | loop fusion | flops 33554432 | bytes 50725888 | tf_op jit(solution)/shard_map/convert_element_type | solution.py:207
  154.5 11.0 %fusion.49 = bf16[256,16,128]{2,1,0:T(8,128)(2,1)S(1)} fusion(f32[256,128,128]{2,1,0:T(8,128)} %bitcast.136, s32[256,128]{1,0:T(8,128)S(1)} %bitcast_subtract_fusion.1), kind=kOutput, calls=%fused_computation.95 | convolution fusion | flops 806354944 | bytes 17956864 | tf_op jit(solution)/shard_map/bew,bel->bwl/dot_general | solution.py:84
  169.7 2.9 convert_reduce_fusion.4
  172.6 1.5 convolution_bitcast_fusion
  174.1 2.2 convert_reduce_fusion.5
  177.8 2.1 convert_reduce_fusion.6
  182.9 1.6 fusion.78
  184.5 16.5 %fusion.47 = f32[256,128,128]{2,1,0:T(8,128)} fusion(f32[256,16,128]{2,1,0:T(8,128)S(1)} %bitcast.157, s32[256,128]{1,0:T(8,128)S(1)} %bitcast_subtract_fusion.1), kind=kOutput, calls=%fused_computation.92 | convolution fusion | flops 805830656 | bytes 19005440 | tf_op jit(solution)/shard_map/bew,bwl->bel/dot_general | solution.py:69
  201.0 28.2 %multiply_reduce_fusion = (f32[128]{0:T(128)}, f32[32768]{0:T(1024)S(1)}, f32[32768]{0:T(1024)S(1)}, f32[128]{0:T(128)}, f32[32768,128]{1,0:T(8,128)}) fusion(f32[32768,128]{1,0:T(8,128)S(1)} %copy-done, f32[32768]{0:T(1024)S(1)} %add_rsqrt_fusion, f32[32768]{0:T(1024)S(1)} %broadcast_multiply_fusion.5, f32[128]{0:T(128)S(1)} %get-tuple-element.175, ...), kind=kLoop, calls=%fused_computation.29 | loop fusion | flops 50265856 | bytes 59377152 | tf_op jit(solution)/shard_map/reduce_sum | solution.py:235
  229.2 21.6 %convert_reduce_fusion = (f32[128]{0:T(128)}, bf16[32768,128]{1,0:T(8,128)(2,1)S(1)}) fusion(f32[32768]{0:T(1024)S(1)} %broadcast_multiply_fusion.3, f32[32768,128]{1,0:T(8,128)S(1)} %copy-done, f32[32768]{0:T(1024)S(1)} %broadcast_multiply_fusion.5, f32[32768]{0:T(1024)S(1)} %broadcast_multiply_fusion.4, f32[32768,128]{1,0:T(8,128)} %get-tuple-element.157, ...), kind=kLoop, calls=%fused_computation.30 | loop fusion | flops 41942912 | bytes 42468352 | tf_op jit(solution)/shard_map/reduce_sum | solution.py:54
  250.9 10.0 %convolution_bitcast_fusion.3 = f32[1,128,128]{2,1,0:T(8,128)} fusion(bf16[32768,128]{1,0:T(8,128)(2,1)S(1)} %get-tuple-element.156, f32[32768,128]{1,0:T(8,128)} %convolution_add_fusion.1), kind=kOutput, calls=%fused_computation.100 | convolution fusion | flops 1111490560 | bytes 25231360 | tf_op jit(solution)/shard_map/dot_general | solution.py:32
  260.9 15.4 %convert_reduce_fusion.1 = (f32[128]{0:T(128)}, bf16[32768,128]{1,0:T(8,128)(2,1)S(1)}) fusion(f32[32768,128]{1,0:T(8,128)} %convolution_add_fusion.1, bf16[32768,128]{1,0:T(8,128)(2,1)S(1)} %get-tuple-element.156, bf16[4,128,128]{2,1,0:T(8,128)(2,1)S(1)} %copy-done.29), kind=kOutput, calls=%fused_computation.31 | convolution fusion | flops 1166016384 | bytes 33587712 | tf_op jit(solution)/shard_map/dot_general | solution.py:26
  276.3 3.3 copy-done.46
  279.6 10.1 %convolution_bitcast_fusion.4 = f32[1,128,128]{2,1,0:T(8,128)} fusion(bf16[32768,128]{1,0:T(8,128)(2,1)S(1)} %get-tuple-element.187, f32[32768,128]{1,0:T(8,128)} %fusion), kind=kOutput, calls=%fused_computation.101 | convolution fusion | flops 1111490560 | bytes 25231360 | tf_op jit(solution)/shard_map/dot_general | solution.py:32
  289.7 16.9 %convert_reduce_fusion.2 = (f32[128]{0:T(128)}, bf16[32768,128]{1,0:T(8,128)(2,1)S(1)}) fusion(f32[32768,128]{1,0:T(8,128)} %fusion, bf16[32768,128]{1,0:T(8,128)(2,1)} %copy-done.46, bf16[4,128,128]{2,1,0:T(8,128)(2,1)S(1)} %copy-done.29), kind=kOutput, calls=%fused_computation.32 | convolution fusion | flops 1166016384 | bytes 33587712 | tf_op jit(solution)/shard_map/dot_general | solution.py:26
  306.6 3.0 fusion.84
  309.6 7.8 %fusion.83 = f32[128,128]{1,0:T(8,128)} fusion(bf16[32768,128]{1,0:T(8,128)(2,1)} %bitcast.145, bf16[32768,128]{1,0:T(8,128)(2,1)S(1)} %get-tuple-element.185), kind=kOutput, calls=%fused_computation.185 | convolution fusion | flops 1073741824 | bytes 16842752 | tf_op jit(solution)/shard_map/dot_general | solution.py:32
  317.5 3.3 convolution_bitcast_fusion.5
  320.7 21.8 %fusion.82 = f32[32768,384]{1,0:T(8,128)} fusion(bf16[32768,128]{1,0:T(8,128)(2,1)} %copy-done.1, bf16[384,128]{1,0:T(8,128)(2,1)} %copy-done.19), kind=kOutput, calls=%fused_computation.184 | convolution fusion | flops 3221225472 | bytes 58818560 | tf_op jit(solution)/shard_map/dot_general | solution.py:26
  343.9 1.8 copy.71
  345.7 35.9 %convert_add_fusion = (f32[32768,128]{1,0:T(8,128)}, f32[32768,128]{1,0:T(8,128)}, f32[32768,128]{1,0:T(8,128)}) fusion(bf16[32768,128]{1,0:T(8,128)(2,1)} %param.31, f32[32768,384]{1,0:T(8,128)} %fusion.82), kind=kLoop, calls=%fused_computation.12 | loop fusion | flops 8388608 | bytes 109051904 | tf_op jit(solution)/shard_map/add | solution.py:253
  381.8 11.6 %convolution_convert_fusion.2 = bf16[256,8,128]{2,1,0:T(8,128)(2,1)} fusion(f32[256,128,128]{2,1,0:T(8,128)} %bitcast.150, s32[256,128]{1,0:T(8,128)S(1)} %copy-done.12), kind=kOutput, calls=%fused_computation.96 | convolution fusion | flops 403177472 | bytes 17432576 | tf_op jit(solution)/shard_map/bew,bel->bwl/dot_general | solution.py:84
  393.4 4.1 all-to-all-start.2
  399.8 11.0 %fusion.46 = f32[256,16,128]{2,1,0:T(8,128)S(1)} fusion(f32[256,128,128]{2,1,0:T(8,128)} %bitcast.137, s32[256,128]{1,0:T(8,128)S(1)} %copy-done.8), kind=kOutput, calls=%fused_computation.91 | convolution fusion | flops 805830656 | bytes 19005440 | tf_op jit(solution)/shard_map/bew,bel->bwl/dot_general | solution.py:84
  410.8 1.8 copy.66
  414.0 41.0 %psum.31 = f32[10,128]{1,0:T(8,128)S(1)} all-reduce(f32[10,128]{1,0:T(8,128)S(1)} %stack.63), channel_id=1, replica_groups=mesh['grp'=4,'dom'=8] {'grp','dom'}, use_global_device_ids=true, to_apply=%region_24.25 | all-reduce | flops 1280 | bytes 10240 | tf_op jit(solution)/shard_map/psum | solution.py:281
  455.6 79.7 %all-reduce.3.cloned.1.call-done = (f32[384,128]{1,0:T(8,128)}, f32[256,128]{1,0:T(8,128)}, f32[4,128,128]{2,1,0:T(8,128)}) async-done(((f32[384,128]{1,0:T(8,128)}, f32[256,128]{1,0:T(8,128)}, f32[4,128,128]{2,1,0:T(8,128)}), (f32[384,128]{1,0:T(8,128)}, f32[256,128]{1,0:T(8,128)}, f32[4,128,128]{2,1,0:T(8,128)})) %all-reduce.3.cloned.1.call-update) | async-done | bytes 589840 | tf_op jit(solution)/shard_map/psum | solution.py:281
  535.3 1.6 multiply_reduce_fusion.5
  537.0 1.5 multiply_reduce_fusion.7
  538.5 1.6 multiply_reduce_fusion.6
  544.7 1.9 multiply_add_fusion.4
  548.0 2.3 multiply_add_fusion.2
  551.6 2.3 multiply_add_fusion
  555.3 9.5 %fusion.21 = f32[4096,128]{0,1:T(8,128)S(1)} fusion(bf16[2048,128]{1,0:T(8,128)(2,1)} %bitcast.31, s32[2048]{0:T(1024)} %bitcast.160, f32[4096,128]{0,1:T(8,128)} %copy.66, f32[4096,128]{0,1:T(8,128)} %copy.71, bf16[4096,128]{0,1:T(8,128)(2,1)S(1)} %copy-done.4), kind=kOutput, calls=%fused_computation.50 | convolution fusion | flops 2157969408 | bytes 7872512 | tf_op jit(solution)/shard_map/while/body/eval_jaxpr/dot_general | solution.py:32
  564.8 1.8 copy.69
  (161 shorter events, 29.3 us)
Async XLA Ops:
  8.5 29.3 %all-to-all-start = ((s32[8,1,256]{2,1,0:T(1,128)}), s32[8,1,256]{2,1,0:T(1,128)S(1)}, u32[]{:S(2)}, u32[]{:S(2)}) async-start(s32[8,1,256]{2,1,0:T(1,128)} %all_to_all.12), calls=%async_computation | async-start | bytes 16384 | tf_op jit(solution)/shard_map/all_to_all | solution.py:181
  16.7 72.1 %copy-start.19 = (bf16[384,128]{1,0:T(8,128)(2,1)}, bf16[384,128]{1,0:T(8,128)(2,1)S(1)}, u32[]{:S(2)}) copy-start(bf16[384,128]{1,0:T(8,128)(2,1)S(1)} %convert_element_type.134) | copy-start | bytes 294916
  17.8 166.8 %copy-start.7 = (s32[256,128]{1,0:T(8,128)}, s32[256,128]{1,0:T(8,128)S(1)}, u32[]{:S(2)}) copy-start(s32[256,128]{1,0:T(8,128)S(1)} %bitcast_subtract_fusion.1) | copy-start | bytes 393220
  18.8 46.5 %copy-start.11 = (s32[256,128]{1,0:T(8,128)}, s32[256,128]{1,0:T(8,128)S(1)}, u32[]{:S(2)}) copy-start(s32[256,128]{1,0:T(8,128)S(1)} %bitcast_subtract_fusion) | copy-start | bytes 393220
  21.9 12.0 %copy-start.35 = (f32[10,128]{1,0:T(8,128)S(1)}, f32[10,128]{1,0:T(8,128)}, u32[]{:S(2)}) copy-start(f32[10,128]{1,0:T(8,128)} %param.44) | copy-start | bytes 15364
  21.9 12.6 %copy-start.2 = (bf16[4096,128]{1,0:T(8,128)(2,1)S(1)}, bf16[4096,128]{1,0:T(8,128)(2,1)}, u32[]{:S(2)}) copy-start(bf16[4096,128]{1,0:T(8,128)(2,1)} %param.24) | copy-start | bytes 3145732
  21.9 14.5 %copy-start.15 = (f32[4,128,128]{2,1,0:T(8,128)S(1)}, f32[4,128,128]{2,1,0:T(8,128)}, u32[]{:S(2)}) copy-start(f32[4,128,128]{2,1,0:T(8,128)} %param.40) | copy-start | bytes 786436
  21.9 14.6 %copy-start.18 = (bf16[4096,128]{1,0:T(8,128)(2,1)S(1)}, bf16[4096,128]{1,0:T(8,128)(2,1)}, u32[]{:S(2)}) copy-start(bf16[4096,128]{1,0:T(8,128)(2,1)} %param.30) | copy-start | bytes 3145732
  36.4 75.9 %copy-start.28 = (bf16[4,128,128]{2,1,0:T(8,128)(2,1)}, bf16[4,128,128]{2,1,0:T(8,128)(2,1)S(1)}, u32[]{:S(2)}) copy-start(bf16[4,128,128]{2,1,0:T(8,128)(2,1)S(1)} %convert_element_type.141) | copy-start | bytes 393220
  44.4 20.9 %all-to-all-start.1 = ((bf16[8,256,128]{2,1,0:T(8,128)(2,1)}), bf16[8,256,128]{2,1,0:T(8,128)(2,1)S(1)}, u32[]{:S(2)}, u32[]{:S(2)}) async-start(bf16[8,256,128]{2,1,0:T(8,128)(2,1)} %bitcast.4), calls=%async_computation.1 | async-start | bytes 1048576 | tf_op jit(solution)/shard_map/all_to_all | solution.py:183
  65.3 23.5 %slice-start = ((s8[8388608]{0:T(1024)(128)(4,1)}), s8[4194304]{0:T(1024)(128)(4,1)S(1)}, s32[]{:S(2)}) async-start(s8[8388608]{0:T(1024)(128)(4,1)} %bitcast.138), calls=%async_computation.4 | async-start | bytes 8388608
  72.0 16.8 %slice-start.1 = ((s8[8388608]{0:T(1024)(128)(4,1)}), s8[4194304]{0:T(1024)(128)(4,1)S(1)}, s32[]{:S(2)}) async-start(s8[8388608]{0:T(1024)(128)(4,1)} %bitcast.138), calls=%async_computation.5 | async-start | bytes 8388608
  99.6 38.1 %slice-start.4 = ((s8[8388608]{0:T(1024)(128)(4,1)}), s8[4194304]{0:T(1024)(128)(4,1)S(1)}, s32[]{:S(2)}) async-start(s8[8388608]{0:T(1024)(128)(4,1)} %bitcast.146), calls=%async_computation.8 | async-start | bytes 8388608
  112.4 25.4 %slice-start.5 = ((s8[8388608]{0:T(1024)(128)(4,1)}), s8[4194304]{0:T(1024)(128)(4,1)S(1)}, s32[]{:S(2)}) async-start(s8[8388608]{0:T(1024)(128)(4,1)} %bitcast.146), calls=%async_computation.9 | async-start | bytes 8388608
  126.1 11.6 %copy-start = (f32[32768,128]{1,0:T(8,128)S(1)}, f32[32768,128]{1,0:T(8,128)}, u32[]{:S(2)}) copy-start(f32[32768,128]{1,0:T(8,128)} %get-tuple-element.181) | copy-start | bytes 50331652
  126.1 11.6 %copy-start.13 = (f32[32768]{0:T(1024)S(1)}, f32[32768]{0:T(1024)}, u32[]{:S(2)}) copy-start(f32[32768]{0:T(1024)} %fusion.59) | copy-start | bytes 393220
  126.2 11.6 %copy-start.43 = (f32[128]{0:T(128)S(1)}, f32[128]{0:T(128)}, u32[]{:S(2)}) copy-start(f32[128]{0:T(128)} %get-tuple-element.174) | copy-start | bytes 1540
  154.4 11.1 %copy-start.5 = (f32[4096,128]{1,0:T(8,128)S(1)}, f32[4096,128]{1,0:T(8,128)}, u32[]{:S(2)}) copy-start(f32[4096,128]{1,0:T(8,128)} %fusion.65) | copy-start | bytes 6291460
  154.4 11.1 %copy-start.42 = (f32[128]{0:T(128)S(1)}, f32[128]{0:T(128)}, u32[]{:S(2)}) copy-start(f32[128]{0:T(128)} %get-tuple-element.173) | copy-start | bytes 1540
  154.4 11.5 %copy-start.29 = (bf16[4,128,128]{2,1,0:T(8,128)(2,1)S(1)}, bf16[4,128,128]{2,1,0:T(8,128)(2,1)}, u32[]{:S(2)}) copy-start(bf16[4,128,128]{2,1,0:T(8,128)(2,1)} %copy-done.28) | copy-start | bytes 393220
  154.5 11.5 %copy-start.45 = (f32[128]{0:T(128)S(1)}, f32[128]{0:T(128)}, u32[]{:S(2)}) copy-start(f32[128]{0:T(128)} %get-tuple-element.172) | copy-start | bytes 1540
  182.9 18.1 %slice-start.8 = ((s8[8388608]{0:T(1024)(128)(4,1)}), s8[4194304]{0:T(1024)(128)(4,1)S(1)}, s32[]{:S(2)}) async-start(s8[8388608]{0:T(1024)(128)(4,1)} %bitcast.151), calls=%async_computation.12 | async-start | bytes 8388608
  184.5 16.5 %slice-start.9 = ((s8[8388608]{0:T(1024)(128)(4,1)}), s8[4194304]{0:T(1024)(128)(4,1)S(1)}, s32[]{:S(2)}) async-start(s8[8388608]{0:T(1024)(128)(4,1)} %bitcast.151), calls=%async_computation.13 | async-start | bytes 8388608
  184.5 16.5 %copy-start.14 = (f32[32768]{0:T(1024)S(1)}, f32[32768]{0:T(1024)}, u32[]{:S(2)}) copy-start(f32[32768]{0:T(1024)} %fusion.59) | copy-start | bytes 393220
  279.6 27.0 %slice-start.2 = ((s8[8388608]{0:T(1024)(128)(4,1)}), s8[4194304]{0:T(1024)(128)(4,1)S(1)}, s32[]{:S(2)}) async-start(s8[8388608]{0:T(1024)(128)(4,1)} %bitcast.141), calls=%async_computation.6 | async-start | bytes 8388608
  289.6 16.9 %slice-start.3 = ((s8[8388608]{0:T(1024)(128)(4,1)}), s8[4194304]{0:T(1024)(128)(4,1)S(1)}, s32[]{:S(2)}) async-start(s8[8388608]{0:T(1024)(128)(4,1)} %bitcast.141), calls=%async_computation.7 | async-start | bytes 8388608
  320.7 21.8 %copy-start.10 = (bf16[4096,128]{0,1:T(8,128)(2,1)S(1)}, bf16[4096,128]{0,1:T(8,128)(2,1)}, u32[]{:S(2)}) copy-start(bf16[4096,128]{0,1:T(8,128)(2,1)} %get-tuple-element.165) | copy-start | bytes 3145732
  320.7 23.1 %copy-start.6 = (f32[4096,128]{1,0:T(8,128)S(1)}, f32[4096,128]{1,0:T(8,128)}, u32[]{:S(2)}) copy-start(f32[4096,128]{1,0:T(8,128)} %get-tuple-element.163) | copy-start | bytes 6291460
  345.7 35.9 %copy-start.12 = (s32[256,128]{1,0:T(8,128)S(1)}, s32[256,128]{1,0:T(8,128)}, u32[]{:S(2)}) copy-start(s32[256,128]{1,0:T(8,128)} %copy-done.11) | copy-start | bytes 393220
  381.6 15.9 %copy-start.26 = (f32[128,128]{1,0:T(8,128)S(1)}, f32[128,128]{1,0:T(8,128)}, u32[]{:S(2)}) copy-start(f32[128,128]{1,0:T(8,128)} %fusion.85) | copy-start | bytes 196612
  381.7 15.9 %copy-start.27 = (f32[128,128]{1,0:T(8,128)S(1)}, f32[128,128]{1,0:T(8,128)}, u32[]{:S(2)}) copy-start(f32[128,128]{1,0:T(8,128)} %convolution_bitcast_fusion.2) | copy-start | bytes 196612
  381.7 16.6 %copy-start.23 = (f32[128,128]{1,0:T(8,128)S(1)}, f32[128,128]{1,0:T(8,128)}, u32[]{:S(2)}) copy-start(f32[128,128]{1,0:T(8,128)} %fusion.84) | copy-start | bytes 196612
  381.7 16.6 %copy-start.24 = (f32[128,128]{1,0:T(8,128)S(1)}, f32[128,128]{1,0:T(8,128)}, u32[]{:S(2)}) copy-start(f32[128,128]{1,0:T(8,128)} %fusion.83) | copy-start | bytes 196612
  381.7 16.6 %copy-start.25 = (f32[128,128]{1,0:T(8,128)S(1)}, f32[128,128]{1,0:T(8,128)}, u32[]{:S(2)}) copy-start(f32[128,128]{1,0:T(8,128)} %convolution_bitcast_fusion.5) | copy-start | bytes 196612
  381.7 17.2 %copy-start.30 = (f32[1,128,128]{2,1,0:T(8,128)S(1)}, f32[1,128,128]{2,1,0:T(8,128)}, u32[]{:S(2)}) copy-start(f32[1,128,128]{2,1,0:T(8,128)} %convolution_bitcast_fusion) | copy-start | bytes 196612
  381.7 17.2 %copy-start.31 = (f32[1,128,128]{2,1,0:T(8,128)S(1)}, f32[1,128,128]{2,1,0:T(8,128)}, u32[]{:S(2)}) copy-start(f32[1,128,128]{2,1,0:T(8,128)} %convolution_bitcast_fusion.1) | copy-start | bytes 196612
  381.7 17.2 %copy-start.32 = (f32[1,128,128]{2,1,0:T(8,128)S(1)}, f32[1,128,128]{2,1,0:T(8,128)}, u32[]{:S(2)}) copy-start(f32[1,128,128]{2,1,0:T(8,128)} %convolution_bitcast_fusion.3) | copy-start | bytes 196612
  381.7 17.2 %copy-start.33 = (f32[1,128,128]{2,1,0:T(8,128)S(1)}, f32[1,128,128]{2,1,0:T(8,128)}, u32[]{:S(2)}) copy-start(f32[1,128,128]{2,1,0:T(8,128)} %convolution_bitcast_fusion.4) | copy-start | bytes 196612
  381.8 18.0 %copy-start.8 = (s32[256,128]{1,0:T(8,128)S(1)}, s32[256,128]{1,0:T(8,128)}, u32[]{:S(2)}) copy-start(s32[256,128]{1,0:T(8,128)} %copy-done.7) | copy-start | bytes 393220
  393.4 161.9 %all-to-all-start.2 = ((bf16[8,256,128]{2,1,0:T(8,128)(2,1)}), bf16[8,256,128]{2,1,0:T(8,128)(2,1)}, u32[]{:S(2)}, u32[]{:S(2)}) async-start(bf16[8,256,128]{2,1,0:T(8,128)(2,1)} %bitcast.30), calls=%async_computation.2 | async-start | bytes 1048576 | tf_op jit(solution)/shard_map/all_to_all | solution.py:258
  397.5 137.8 %all-reduce.3.cloned.1.call-start = ((), (), s32[]{:S(2)}) async-start(), calls=%async_computation.3 | async-start | bytes 1179648 | tf_op jit(solution)/shard_map/psum | solution.py:281
  399.7 12.9 %copy-start.39 = (f32[128]{0:T(128)S(1)}, f32[128]{0:T(128)}, u32[]{:S(2)}) copy-start(f32[128]{0:T(128)} %get-tuple-element.130) | copy-start | bytes 1540
  399.7 12.9 %copy-start.40 = (f32[128]{0:T(128)S(1)}, f32[128]{0:T(128)}, u32[]{:S(2)}) copy-start(f32[128]{0:T(128)} %get-tuple-element.133) | copy-start | bytes 1540
  399.7 143.0 %copy-start.36 = (f32[10,128]{1,0:T(8,128)S(1)}, f32[10,128]{1,0:T(8,128)}, u32[]{:S(2)}) copy-start(f32[10,128]{1,0:T(8,128)} %param.44) | copy-start | bytes 15364
  399.8 145.0 %copy-start.21 = (f32[256,128]{1,0:T(8,128)S(1)}, f32[256,128]{1,0:T(8,128)}, u32[]{:S(2)}) copy-start(f32[256,128]{1,0:T(8,128)} %param.36) | copy-start | bytes 393220
  410.8 140.8 %copy-start.16 = (f32[4,128,128]{2,1,0:T(8,128)S(1)}, f32[4,128,128]{2,1,0:T(8,128)}, u32[]{:S(2)}) copy-start(f32[4,128,128]{2,1,0:T(8,128)} %param.40) | copy-start | bytes 786436
  410.8 144.5 %copy-start.4 = (bf16[4096,128]{0,1:T(8,128)(2,1)S(1)}, bf16[4096,128]{0,1:T(8,128)(2,1)}, u32[]{:S(2)}) copy-start(bf16[4096,128]{0,1:T(8,128)(2,1)} %copy.64) | copy-start | bytes 3145732
  544.1 20.7 %copy-start.34 = (f32[10,128]{1,0:T(8,128)}, f32[10,128]{1,0:T(8,128)S(1)}, u32[]{:S(2)}) copy-start(f32[10,128]{1,0:T(8,128)S(1)} %get-tuple-element.142) | copy-start | bytes 15364
  (13 other events, 55.5 us)
Sparse Core Ops, SparseCore 0:
  405.1 130.1 all-reduce.2
where the time goes:
time: 583 us; the launch traced here: 575 us
  matrix products  250 us (43%)
  other arithmetic  141 us (24%)
  waiting for transfers between devices  87.7 us (15%)
  blocking collectives  41 us (7%)
  local copies, waits for them, and re-layouts  19.8 us (3%)
  between operations  19.6 us (3%)
  starting transfers between devices  16.1 us (3%)
    psum x1, waiting for transfers between devices, shards(): lax.psum((grad_edge_entry, grad_node_entry, grad_inner, grad_vectors), ('...  79.7 us
    dot_general x10, matrix products, matmul(): return jnp.dot(operand, weights, preferred_element_type=jnp.float32)  78 us
    dot_general x6, matrix products, matmul_nt(): lax.dot_general(operand, weights, (((1,), (1,)), ((), ())), preferred_ele...  59.3 us
    dot_general x10, matrix products, matmul_tn(): lax.dot_general(operand, weights, (((0,), (0,)), ((), ())), preferred_ele...  49 us
    psum x1, blocking collectives, shards(): lax.psum((grad_edge_entry, grad_node_entry, grad_inner, grad_vectors), ('...  41 us
    add x1, other arithmetic, shards(): edge_grad = edge_upstream + edge_input_grad[:, :width]  35.9 us
    dot_general x3, matrix products, window_add(): jnp.einsum('bew,bel->bwl', onehot, shaped, precision=lax.Precision.HIGHES...  33.6 us
    reduce_sum x1, other arithmetic, shards(): grad_edge_gain = jnp.sum(message_grad * edge_normed, axis=0)  28.2 us
  transfers between devices with their start and end apart: 4, of which 2 were waited for; matrix products, arithmetic and copies ran while one was open for 11% of the time, Pallas kernels for 0%

commit v1 on v0

v1 whole, which is shorter than its diff:
```python
import functools
import math

import jax
import jax.numpy as jnp
from jax import lax
from jax.experimental import pallas as pl
from jax.experimental.pallas import tpu as pltpu
from jax.sharding import PartitionSpec as P

STEP = 10

eps_norm = 1e-05
beta_one = 0.5
beta_two = 0.6
learn_rate = 0.08
decay_rate = 0.01
adam_eps = 1e-08
ema_keep = 0.9
clip_level = 1.0

gelu_in = math.sqrt(2.0 / math.pi)
gelu_cube = gelu_in * 0.044715

low = jnp.bfloat16
high = jnp.float32

GAP = 4
VMEM = 60 * 1024 * 1024
PAIRS = 8


def dot(operand, weights):
    return jnp.dot(operand, weights, preferred_element_type=high)


def dot_nt(operand, weights):
    return lax.dot_general(
        operand, weights, (((1,), (1,)), ((), ())), preferred_element_type=high
    )


def dot_tn(operand, weights):
    return lax.dot_general(
        operand, weights, (((0,), (0,)), ((), ())), preferred_element_type=high
    )


def gelu_pair(x):
    square = x * x
    u = x * (gelu_in + gelu_cube * square)
    s = 0.5 + 0.5 * jnp.tanh(u)
    value = x * s
    slope = s + (value - value * s) * (2.0 * gelu_in + (6.0 * gelu_cube) * square)
    return value, slope


def fold_rows(values):
    return jnp.sum(values.reshape(values.shape[0] // 8, 8, values.shape[1]), axis=0)


def emit(pairs, per_group, forward, middle, backward, end):
    groups = pairs // per_group
    streams = {"forward": forward, "middle": middle, "backward": backward, "end": end}
    started = dict.fromkeys(streams, 0)
    last = dict.fromkeys(streams, -GAP)
    active, done, now = [], set(), 0

    def ready(name, k):
        if name == "middle":
            return all(("forward", k * per_group + j) in done for j in range(per_group))
        if name == "end":
            return all(("backward", k * per_group + j) in done for j in range(per_group))
        return name == "forward" or ("middle", k // per_group) in done

    while len(done) < 2 * pairs + 2 * groups:
        for name in streams:
            k = started[name]
            count = pairs if name in ("forward", "backward") else groups
            if k < count and now - last[name] >= GAP and ready(name, k):
                active.append(((name, k), streams[name](k)))
                started[name], last[name] = k + 1, now
        for item in list(active):
            try:
                next(item[1])
            except StopIteration:
                active.remove(item)
                done.add(item[0])
        now += 1


class Sizes:
    def __init__(self, edges, nodes, slots, devices):
        self.edges, self.nodes, self.slots = edges, nodes, slots
        blocks = edges // 128
        self.rwin = nodes // blocks
        self.swin = slots // blocks
        self.sub = 4
        while self.sub * (self.rwin + self.swin) > 128:
            self.sub //= 2
        self.chunk = self.sub * 128
        self.chunk_slots = self.sub * self.swin
        self.chunk_nodes = self.sub * self.rwin
        self.pair_nodes, self.pair_slots = 2 * self.chunk_nodes, 2 * self.chunk_slots
        self.per_group = 4
        self.pairs = PAIRS
        self.group_nodes = self.per_group * self.pair_nodes
        self.group_slots = self.per_group * self.pair_slots
        self.tile = self.pairs * 2 * self.chunk
        self.tile_chunks = 2 * self.pairs
        self.tile_nodes = self.pairs * self.pair_nodes
        self.tile_slots = self.pairs * self.pair_slots
        self.steps = edges // self.tile
        self.grad_rows = -(-1162 // (16 * devices)) * 16 * devices


def diagonal(first, second):
    zero_a = jnp.zeros((first.shape[0], second.shape[1]), first.dtype)
    zero_b = jnp.zeros((second.shape[0], first.shape[1]), first.dtype)
    return jnp.concatenate(
        [
            jnp.concatenate([first, zero_a], axis=1),
            jnp.concatenate([zero_b, second], axis=1),
        ],
        axis=0,
    )


def twice(row):
    return jnp.concatenate([row, row], axis=1)


def layer_kernel(
    z,
    count_ref,
    slot_ids_ref,
    recv_ids_ref,
    edge_in_ref,
    edge_cot_ref,
    node_in_ref,
    node_cot_ref,
    slot_ref,
    edge_entry_ref,
    node_entry_ref,
    inner_ref,
    vec_ref,
    node_out_ref,
    edge_out_ref,
    node_grad_ref,
    edge_grad_ref,
    slot_grad_ref,
    grads_ref,
    pick_s,
    pick_t,
    act_one_s,
    act_two_s,
    slope_one_s,
    slope_two_s,
    normed_s,
    inverse_s,
    gathered_s,
    table_s,
    slot_pre_s,
    node_pre_s,
    slot_sum_s,
    recv_sum_s,
    sums_s,
    wide_s,
    below_s,
):
    step = pl.program_id(0)
    chunk, cn, cs = z.chunk, z.chunk_nodes, z.chunk_slots
    pad = 128 - cn - cs
    vec = [vec_ref[pl.ds(k, 1), :] for k in range(10)]

    @pl.when(step == 0)
    def _():
        grads_ref[...] = jnp.zeros_like(grads_ref)
        sums_s[...] = jnp.zeros_like(sums_s)
        first, second = inner_ref[0].astype(low), inner_ref[1].astype(low)
        wide_s[0] = diagonal(first, first)
        middle = second.astype(high)
        middle = (middle - jnp.mean(middle, axis=1, keepdims=True)).astype(low)
        wide_s[1] = diagonal(middle, middle)
        for k, weights in ((2, inner_ref[0]), (3, inner_ref[1]), (4, edge_entry_ref[0:128, :])):
            weights = weights.T.astype(low)
            wide_s[k] = diagonal(weights, weights)
        part = jnp.full((128, 128), 1.0 / 128.0, low)
        wide_s[5] = diagonal(part, part)
        row = lax.broadcasted_iota(jnp.int32, (128, 128), 0)
        column = lax.broadcasted_iota(jnp.int32, (128, 128), 1)
        gain = jnp.broadcast_to(vec[3] * (1.0 / 128.0), (128, 128)).T.astype(low)
        wide_s[6] = diagonal(gain, gain)
        below_s[:, :128] = jnp.where(row == column, 1.0, 0.0).astype(low)
        below_s[:, 128:] = gain

    edge_low = edge_entry_ref[...].astype(low)
    node_low = node_entry_ref[...].astype(low)
    inner_low = [None, None, inner_ref[2].astype(low), inner_ref[3].astype(low)]
    w_edge, w_slot, w_recv = edge_low[:128], edge_low[128:256], edge_low[256:]
    bias_three = vec[2] - jnp.mean(vec[2], axis=1, keepdims=True)
    gain_part = below_s[:, 128:]
    row_ids = lax.broadcasted_iota(jnp.int32, (chunk, 128), 0)
    slot_pre_s[...] = dot(slot_ref[...], w_slot).astype(low)
    node_pre_s[...] = (dot(node_in_ref[...], w_recv) + vec[0]).astype(low)

    def live_rows(index):
        return row_ids < count_ref[0] - (step * z.tile + index * chunk)

    def sides(wide):
        return wide[:, :128], wide[:, 128:]

    def chunk_rows(index):
        return pl.ds(index * chunk, chunk)

    def hot_columns(index):
        columns = []
        for k in range(z.sub):
            block = index * z.sub + k
            number = step * (z.tile // 128) + block
            pieces = []
            for ref, width, count in ((slot_ids_ref, z.swin, cs), (recv_ids_ref, z.rwin, cn)):
                ids = ref[pl.ds(block, 1), :] - number * width
                band = lax.broadcasted_iota(jnp.int32, (width, 128), 0) == ids
                above, below = k * width, count - (k + 1) * width
                if above:
                    pieces.append(jnp.zeros((above, 128), high))
                pieces.append(jnp.where(band, 1.0, 0.0))
                if below:
                    pieces.append(jnp.zeros((below, 128), high))
            if pad:
                pieces.append(jnp.zeros((pad, 128), high))
            columns.append(jnp.concatenate(pieces, axis=0).astype(low))
        return jnp.concatenate(columns, axis=1)

    def edge_forward(pair):
        wide_rows = chunk_rows(pair)
        indices = (2 * pair, 2 * pair + 1)
        pres = []
        for side, index in enumerate(indices):
            hot_t = hot_columns(index)
            hot = hot_t.T
            pick_t[index] = hot_t
            pick_s[chunk_rows(index), :] = hot
            tables = [
                w_edge,
                slot_pre_s[pl.ds(index * cs, cs), :],
                node_pre_s[pl.ds(index * cn, cn), :],
            ]
            if pad:
                tables.append(jnp.zeros((pad, 128), low))
            rows = edge_in_ref[chunk_rows(index), :]
            pres.append(
                dot(jnp.concatenate([rows, hot], axis=1), jnp.concatenate(tables, axis=0)).astype(low)
            )
            yield
        act_one, slope = gelu_pair(jnp.concatenate(pres, axis=1))
        act_one_s[wide_rows, :] = act_one
        slope_one_s[wide_rows, :] = slope
        yield
        pre_two = (dot(act_one, wide_s[0]) + twice(vec[1])).astype(low)
        yield
        act_two, slope = gelu_pair(pre_two)
        act_two_s[wide_rows, :] = act_two
        slope_two_s[wide_rows, :] = slope
        yield
        center = dot(act_two, wide_s[1]) + twice(bias_three)
        square = (center * center).astype(low)
        yield
        inverse = lax.rsqrt(dot(square, wide_s[5]) + eps_norm)
        yield
        messages = []
        for index, center, inverse in zip(indices, sides(center), sides(inverse)):
            live = live_rows(index)
            inverse = jnp.where(live, inverse, 0.0)
            normed = center * inverse
            normed_s[chunk_rows(index), :] = normed
            inverse_s[chunk_rows(index), :] = inverse
            message = jnp.where(live, normed * vec[3] + vec[4], 0.0)
            rows = edge_in_ref[chunk_rows(index), :]
            edge_out_ref[chunk_rows(index), :] = (rows.astype(high) + message).astype(low)
            messages.append(message.astype(low))
        yield
        hots = [pick_t[index, cs : cs + cn, :] for index in indices]
        total = dot(jnp.concatenate(hots, axis=0), jnp.concatenate(messages, axis=1)).astype(low)
        gathered_s[pl.ds(indices[0] * cn, cn), :] = total[:cn, :128]
        gathered_s[pl.ds(indices[1] * cn, cn), :] = total[cn:, 128:]
        yield

    def node_phase(group):
        rows = pl.ds(group * z.group_nodes, z.group_nodes)
        node_rows = node_in_ref[rows, :]
        entry = jnp.concatenate([node_rows, gathered_s[rows, :]], axis=1)
        node_one = (dot(entry, node_low) + vec[5]).astype(low)
        yield
        act_one, slope_one = gelu_pair(node_one)
        yield
        node_two = (dot(act_one, inner_low[2]) + vec[6]).astype(low)
        yield
        act_two, slope_two = gelu_pair(node_two)
        yield
        node_three = dot(act_two, inner_low[3]) + vec[7]
        yield
        center = node_three - jnp.mean(node_three, axis=1, keepdims=True)
        inverse = lax.rsqrt(jnp.mean(center * center, axis=1, keepdims=True) + eps_norm)
        normed = center * inverse
        node_out_ref[rows, :] = (node_rows.astype(high) + normed * vec[8] + vec[9]).astype(low)
        yield
        upstream = node_cot_ref[rows, :].astype(high)
        sums_s[8] += fold_rows(upstream * normed)
        sums_s[9] += fold_rows(upstream)
        upper = upstream * vec[8]
        mean_plain = jnp.mean(upper, axis=1, keepdims=True)
        mean_cross = jnp.mean(upper * normed, axis=1, keepdims=True)
        d_three = inverse * (upper - mean_plain - normed * mean_cross)
        sums_s[7] += fold_rows(d_three)
        d_three = d_three.astype(low)
        yield
        back = dot_nt(d_three, inner_low[3])
        yield
        d_two = back * slope_two.astype(high)
        sums_s[6] += fold_rows(d_two)
        d_two = d_two.astype(low)
        yield
        back = dot_nt(d_two, inner_low[2])
        yield
        d_one = back * slope_one.astype(high)
        sums_s[5] += fold_rows(d_one)
        d_one = d_one.astype(low)
        yield
        back = dot_nt(d_one, node_low)
        node_grad_ref[rows, :] = upstream + back[:, :128]
        arrived = back[:, 128:].astype(low)
        yield
        table_s[rows, :128] = arrived
        table_s[rows, 128:] = dot(arrived, gain_part).astype(low)
        yield
        grads_ref[384:640, :] += dot_tn(entry, d_one)
        grads_ref[896:1024, :] += dot_tn(act_one, d_two)
        grads_ref[1024:1152, :] += dot_tn(act_two, d_three)
        yield

    def edge_backward(pair):
        wide_rows = chunk_rows(pair)
        indices = (2 * pair, 2 * pair + 1)
        upstreams, plains, crosses = [], [], []
        for index in indices:
            tables = [
                jnp.zeros((cs, 256), low),
                table_s[pl.ds(index * cn, cn), :],
            ]
            if pad:
                tables.append(jnp.zeros((pad, 256), low))
            tables.append(below_s[...])
            entry = jnp.concatenate(
                [pick_s[chunk_rows(index), :], edge_cot_ref[chunk_rows(index), :]], axis=1
            )
            upstream, plain = sides(dot(entry, jnp.concatenate(tables, axis=0)))
            upstreams.append(upstream)
            plains.append(plain)
            yield
        for index, upstream in zip(indices, upstreams):
            cross = upstream * normed_s[chunk_rows(index), :]
            sums_s[3] += fold_rows(cross)
            sums_s[4] += fold_rows(jnp.where(live_rows(index), upstream, 0.0))
            crosses.append(cross.astype(low))
        yield
        means = dot(jnp.concatenate(crosses, axis=1), wide_s[6])
        yield
        threes = []
        for index, upstream, plain, cross in zip(indices, upstreams, plains, sides(means)):
            normed = normed_s[chunk_rows(index), :]
            d_three = inverse_s[chunk_rows(index), :] * (
                upstream * vec[3] - plain - normed * cross
            )
            threes.append(d_three.astype(low))
        d_three = jnp.concatenate(threes, axis=1)
        yield
        d_two = dot(d_three, wide_s[3]).astype(low) * slope_two_s[wide_rows, :]
        yield
        d_one = dot(d_two, wide_s[2]).astype(low) * slope_one_s[wide_rows, :]
        yield
        for index, back in zip(indices, sides(dot(d_one, wide_s[4]))):
            edge_grad_ref[chunk_rows(index), :] = (
                edge_cot_ref[chunk_rows(index), :].astype(high) + back
            )
        yield
        ones = jnp.ones((16, chunk), low)
        entry = [edge_in_ref[chunk_rows(index), :].T for index in indices]
        hots = [pick_t[index, : cs + cn, :] for index in indices]
        total = dot(jnp.concatenate(entry + hots, axis=0), d_one)
        grads_ref[0:128, :] += total[:128, :128] + total[128:256, 128:]
        first = total[256 : 256 + cs + cn, :128]
        second = total[256 + cs + cn :, 128:]
        yield
        node_rows = pl.ds(pair * z.pair_nodes, z.pair_nodes)
        slot_rows = pl.ds(pair * z.pair_slots, z.pair_slots)
        slot_sum_s[slot_rows, :] = jnp.concatenate([first[:cs], second[:cs]], axis=0).astype(low)
        recv_sum = jnp.concatenate([first[cs:], second[cs:]], axis=0)
        sums_s[0] += fold_rows(recv_sum)
        recv_sum_s[node_rows, :] = recv_sum.astype(low)
        yield
        for k, act_s, gradient in ((1, act_one_s, d_two), (2, act_two_s, d_three)):
            total = dot(jnp.concatenate([act_s[wide_rows, :].T, ones], axis=0), gradient)
            grads_ref[pl.ds(512 + 128 * k, 128), :] += total[:128, :128] + total[128:256, 128:]
            sums_s[k] += (total[256:264, :128] + total[256:264, 128:]) * 0.125
            yield

    def group_end(group):
        node_rows = pl.ds(group * z.group_nodes, z.group_nodes)
        slot_rows = pl.ds(group * z.group_slots, z.group_slots)
        slot_grad_ref[slot_rows, :] = dot_nt(slot_sum_s[slot_rows, :], w_slot).astype(low)
        node_grad_ref[node_rows, :] += dot_nt(recv_sum_s[node_rows, :], w_recv)
        yield
        grads_ref[128:256, :] += dot_tn(slot_ref[slot_rows, :], slot_sum_s[slot_rows, :])
        grads_ref[256:384, :] += dot_tn(node_in_ref[node_rows, :], recv_sum_s[node_rows, :])
        yield

    emit(z.pairs, z.per_group, edge_forward, node_phase, edge_backward, group_end)

    @pl.when(step == z.steps - 1)
    def _():
        grads_ref[1152:1162, :] = jnp.sum(sums_s[...], axis=1)


def layer_call(z, count, slot_ids, recv_ids, edge_in, edge_cot, node_in, node_cot, slot_rows, weights):
    def rows_spec(rows):
        return pl.BlockSpec((rows, 128), lambda i: (i, 0))

    def whole(array):
        return pl.BlockSpec(array.shape, lambda i: (0,) * array.ndim)

    return pl.pallas_call(
        functools.partial(layer_kernel, z),
        grid=(z.steps,),
        in_specs=[
            pl.BlockSpec(memory_space=pltpu.SMEM),
            rows_spec(z.tile // 128),
            rows_spec(z.tile // 128),
            rows_spec(z.tile),
            rows_spec(z.tile),
            rows_spec(z.tile_nodes),
            rows_spec(z.tile_nodes),
            rows_spec(z.tile_slots),
        ]
        + [whole(w) for w in weights],
        out_specs=[
            rows_spec(z.tile_nodes),
            rows_spec(z.tile),
            rows_spec(z.tile_nodes),
            rows_spec(z.tile),
            rows_spec(z.tile_slots),
            pl.BlockSpec((z.grad_rows, 128), lambda i: (0, 0)),
        ],
        out_shape=[
            jax.ShapeDtypeStruct((z.nodes, 128), low),
            jax.ShapeDtypeStruct((z.edges, 128), low),
            jax.ShapeDtypeStruct((z.nodes, 128), high),
            jax.ShapeDtypeStruct((z.edges, 128), high),
            jax.ShapeDtypeStruct((z.slots, 128), low),
            jax.ShapeDtypeStruct((z.grad_rows, 128), high),
        ],
        scratch_shapes=[
            pltpu.VMEM((z.tile, 128), low),
            pltpu.VMEM((z.tile_chunks, 128, z.chunk), low),
            pltpu.VMEM((z.tile // 2, 256), low),
            pltpu.VMEM((z.tile // 2, 256), low),
            pltpu.VMEM((z.tile // 2, 256), low),
            pltpu.VMEM((z.tile // 2, 256), low),
            pltpu.VMEM((z.tile, 128), high),
            pltpu.VMEM((z.tile, 128), high),
            pltpu.VMEM((z.tile_nodes, 128), low),
            pltpu.VMEM((z.tile_nodes, 256), low),
            pltpu.VMEM((z.tile_slots, 128), low),
            pltpu.VMEM((z.tile_nodes, 128), low),
            pltpu.VMEM((z.tile_slots, 128), low),
            pltpu.VMEM((z.tile_nodes, 128), low),
            pltpu.VMEM((10, 8, 128), high),
            pltpu.VMEM((7, 256, 256), low),
            pltpu.VMEM((128, 256), low),
        ],
        compiler_params=pltpu.CompilerParams(
            dimension_semantics=("arbitrary",), vmem_limit_bytes=VMEM
        ),
        name="layer",
    )(count, slot_ids, recv_ids, edge_in, edge_cot, node_in, node_cot, slot_rows, *weights)


def signal(semaphore, where):
    pl.semaphore_signal(semaphore, inc=1, device_id=where, device_id_type=pl.DeviceIdType.MESH)


def send(source, target, send_sem, recv_sem, where):
    copy = pltpu.make_async_remote_copy(
        src_ref=source,
        dst_ref=target,
        send_sem=send_sem,
        recv_sem=recv_sem,
        device_id=where,
        device_id_type=pl.DeviceIdType.MESH,
    )
    copy.start()
    return copy


def fetch_kernel(
    peers,
    unroll,
    request_ref,
    node_ref,
    rows_ref,
    asked_ref,
    wanted_v,
    asked_v,
    node_v,
    node_s,
    picked_s,
    out_s,
    ask_send,
    ask_recv,
    row_send,
    row_recv,
    load_sem,
):
    me = lax.axis_index("dom")
    slots = picked_s.shape[0]
    barrier = pltpu.get_barrier_semaphore()
    for k in range(1, peers):
        signal(barrier, {"dom": lax.rem(me + k, peers)})
    loads = [
        pltpu.make_async_copy(request_ref, wanted_v, load_sem.at[0]),
        pltpu.make_async_copy(node_ref, node_v, load_sem.at[1]),
    ]
    for load in loads:
        load.start()
    loads[0].wait()
    for k in range(peers):
        asked_v[k] = wanted_v[pl.ds(k, 1), :]
    loads[1].wait()
    node_s[...] = node_v[...].astype(high)
    pl.semaphore_wait(barrier, peers - 1)
    shifts = [peers // 2 + (k // 2) * (1 - 2 * (k % 2)) for k in range(1, peers)]
    asks = [
        send(
            asked_v.at[lax.rem(me + k, peers)],
            asked_v.at[peers + me],
            ask_send.at[k],
            ask_recv.at[k],
            {"dom": lax.rem(me + k, peers)},
        )
        for k in shifts
    ]
    asked_v[peers + me] = asked_v[me]
    for ask in asks:
        ask.wait_recv()
    local = pltpu.make_async_copy(asked_v.at[pl.ds(peers, peers)], asked_ref, load_sem.at[0])
    local.start()
    local.wait()
    sends = []
    for k in shifts + [0]:
        other = lax.rem(me + (peers - k), peers)

        @pl.loop(0, slots // unroll)
        def _(group):
            for place in range(unroll):
                row = group * unroll + place
                index = asked_ref[other, 0, row]
                picked_s[pl.ds(row, 1), :] = node_s[pl.ds(index, 1), :]

        out_s[other] = picked_s[...].astype(low)
        if k:
            sends.append(
                send(
                    out_s.at[other],
                    rows_ref.at[me],
                    row_send.at[k],
                    row_recv.at[k],
                    {"dom": other},
                )
            )
    local = pltpu.make_async_copy(out_s.at[me], rows_ref.at[me], load_sem.at[0])
    local.start()
    for copy in asks:
        copy.wait_send()
    local.wait()
    for copy in sends:
        copy.wait()


def fetch_call(peers, request, node_in):
    slots = request.shape[2]
    dma = pltpu.SemaphoreType.DMA
    hbm = pl.BlockSpec(memory_space=pltpu.HBM)
    return pl.pallas_call(
        functools.partial(fetch_kernel, peers, 32),
        in_specs=[hbm, hbm],
        out_specs=[hbm, pl.BlockSpec(memory_space=pltpu.SMEM)],
        out_shape=[
            jax.ShapeDtypeStruct((peers, slots, 128), low),
            jax.ShapeDtypeStruct((peers, 1, slots), jnp.int32),
        ],
        scratch_shapes=[
            pltpu.VMEM((peers, slots), jnp.int32),
            pltpu.VMEM((2 * peers, 1, slots), jnp.int32),
            pltpu.VMEM(node_in.shape, low),
            pltpu.VMEM(node_in.shape, high),
            pltpu.VMEM((slots, 128), high),
            pltpu.VMEM((peers, slots, 128), low),
            dma((peers,)),
            dma((peers,)),
            dma((peers,)),
            dma((peers,)),
            dma((2,)),
        ],
        compiler_params=pltpu.CompilerParams(
            collective_id=0, has_side_effects=True, vmem_limit_bytes=VMEM
        ),
        name="fetch",
    )(request.reshape(peers, slots), node_in)


def reduce_kernel(
    groups,
    peers,
    grads_ref,
    slot_grad_ref,
    sum_ref,
    back_ref,
    grads_s,
    all_s,
    half_out,
    half_in,
    half_sum,
    quarter_out,
    quarter_in,
    quarter_sum,
    piece_out,
    piece_in,
    back_send,
    back_recv,
    half_send,
    half_recv,
    quarter_send,
    quarter_recv,
    piece_send,
    piece_recv,
    load_sem,
):
    grp, dom = lax.axis_index("grp"), lax.axis_index("dom")
    core, level = lax.rem(dom, 2), lax.div(dom, 2)
    levels = peers // 2
    half, quarter, piece = half_sum.shape[0], quarter_sum.shape[0], piece_out.shape[1]
    barrier = pltpu.get_barrier_semaphore()
    for k in range(1, peers):
        signal(barrier, {"dom": lax.rem(dom + k, peers)})
    for k in range(1, groups):
        signal(barrier, {"grp": lax.rem(grp + k, groups)})
    twin = {"dom": 2 * level + 1 - core}
    loads = [
        pltpu.make_async_copy(
            grads_ref.at[pl.ds(first, half), :], grads_s.at[pl.ds(first, half), :], load_sem.at[k]
        )
        for k, first in enumerate(((1 - core) * half, core * half))
    ]
    loads.append(
        pltpu.make_async_copy(slot_grad_ref.at[dom], back_ref.at[dom], load_sem.at[2])
    )
    for load in loads:
        load.start()
    loads[0].wait()
    half_out[...] = grads_s[pl.ds((1 - core) * half, half), :].astype(low)
    loads[1].wait()
    pl.semaphore_wait(barrier, peers - 1 + groups - 1)

    sends = [send(half_out, half_in, half_send.at[0], half_recv.at[0], twin)]

    def give_back(k):
        other = lax.rem(dom + k, peers)
        return send(
            slot_grad_ref.at[other],
            back_ref.at[dom],
            back_send.at[k],
            back_recv.at[k],
            {"dom": other},
        )

    early = [k for k in range(1, peers) if 2 * k == peers or (2 * k < peers and k % 2)]
    backs = [give_back(k) for k in early]
    sends[0].wait_recv()
    half_sum[...] = grads_s[pl.ds(core * half, half), :] + half_in[...].astype(high)

    copies = []
    for k in range(1, groups):
        other = lax.rem(grp + k, groups)
        quarter_out[k] = half_sum[pl.ds(other * quarter, quarter), :].astype(low)
        copies.append(
            send(
                quarter_out.at[k],
                quarter_in.at[k],
                quarter_send.at[k],
                quarter_recv.at[k],
                {"grp": other},
            )
        )
    total = half_sum[pl.ds(grp * quarter, quarter), :]
    for k in range(1, groups):
        copies[k - 1].wait_recv()
        total = total + quarter_in[k].astype(high)
    quarter_sum[...] = total
    sends += copies

    copies = []
    for k in range(1, levels):
        other = lax.rem(level + k, levels)
        piece_out[k] = quarter_sum[pl.ds(other * piece, piece), :].astype(low)
        copies.append(
            send(
                piece_out.at[k],
                piece_in.at[k],
                piece_send.at[k],
                piece_recv.at[k],
                {"dom": 2 * other + core},
            )
        )
    total = quarter_sum[pl.ds(level * piece, piece), :]
    for k in range(1, levels):
        copies[k - 1].wait_recv()
        total = total + piece_in[k].astype(high)
    sends += copies

    own_half = core * half
    own_quarter = own_half + grp * quarter
    own_piece = own_quarter + level * piece
    all_s[pl.ds(own_piece, piece), :] = total.astype(low)
    copies = []
    for k in range(1, levels):
        place = all_s.at[pl.ds(own_piece, piece), :]
        where = {"dom": 2 * lax.rem(level + k, levels) + core}
        copies.append(
            send(place, place, piece_send.at[levels + k], piece_recv.at[levels + k], where)
        )
    backs += [give_back(k) for k in range(1, peers) if k not in early]
    for copy in copies:
        copy.wait_recv()
    sends += copies
    copies = []
    for k in range(1, groups):
        place = all_s.at[pl.ds(own_quarter, quarter), :]
        where = {"grp": lax.rem(grp + k, groups)}
        copies.append(
            send(place, place, quarter_send.at[groups + k], quarter_recv.at[groups + k], where)
        )
    for copy in copies:
        copy.wait_recv()
    sends += copies
    place = all_s.at[pl.ds(own_half, half), :]
    copy = send(place, place, half_send.at[1], half_recv.at[1], twin)
    copy.wait_recv()
    sends.append(copy)
    loads[2].wait()
    for copy in backs:
        copy.wait()
    for copy in sends:
        copy.wait_send()
    sum_ref[...] = all_s[...]


def reduce_call(groups, peers, grads, slot_grad):
    rows = grads.shape[0]
    levels = peers // 2
    half, quarter, piece = rows // 2, rows // 2 // groups, rows // 2 // groups // levels
    dma = pltpu.SemaphoreType.DMA
    return pl.pallas_call(
        functools.partial(reduce_kernel, groups, peers),
        in_specs=[pl.BlockSpec(memory_space=pltpu.HBM)] * 2,
        out_specs=[
            pl.BlockSpec(memory_space=pltpu.VMEM),
            pl.BlockSpec(memory_space=pltpu.HBM),
        ],
        out_shape=[
            jax.ShapeDtypeStruct((rows, 128), low),
            jax.ShapeDtypeStruct(slot_grad.shape, low),
        ],
        scratch_shapes=[
            pltpu.VMEM((rows, 128), high),
            pltpu.VMEM((rows, 128), low),
            pltpu.VMEM((half, 128), low),
            pltpu.VMEM((half, 128), low),
            pltpu.VMEM((half, 128), high),
            pltpu.VMEM((groups, quarter, 128), low),
            pltpu.VMEM((groups, quarter, 128), low),
            pltpu.VMEM((quarter, 128), high),
            pltpu.VMEM((levels, piece, 128), low),
            pltpu.VMEM((levels, piece, 128), low),
            dma((peers,)),
            dma((peers,)),
            dma((2,)),
            dma((2,)),
            dma((2 * groups,)),
            dma((2 * groups,)),
            dma((2 * levels,)),
            dma((2 * levels,)),
            dma((3,)),
        ],
        compiler_params=pltpu.CompilerParams(
            collective_id=1, has_side_effects=True, vmem_limit_bytes=VMEM
        ),
        name="reduce",
    )(grads, slot_grad)


def adamw_step(master, moment_mean, moment_var, average, gradient, factor):
    clipped = gradient * factor
    mean_new = beta_one * moment_mean + (1.0 - beta_one) * clipped
    var_new = beta_two * moment_var + (1.0 - beta_two) * clipped * clipped
    mean_hat = mean_new / (1.0 - beta_one**STEP)
    var_hat = var_new / (1.0 - beta_two**STEP)
    updated = master - learn_rate * (
        mean_hat / (jnp.sqrt(var_hat) + adam_eps) + decay_rate * master
    )
    return (
        mean_new,
        var_new,
        updated,
        updated.astype(low),
        ema_keep * average + (1.0 - ema_keep) * updated,
    )


FIRST = (0, 384, 640, 1152, 1162)


def finish_kernel(unroll, asked_ref, *refs):
    sources, (norm_ref, *results), refs = refs[:19], refs[19:41], refs[41:]
    loaded, (rows_s, *staged, load_sem, store_sem) = refs[:19], refs[19:]
    summed_s, back_s, node_s = loaded[16:]
    loads = [
        pltpu.make_async_copy(source, place, load_sem.at[k])
        for k, (source, place) in enumerate(zip(sources, loaded))
    ]
    for load in [*loads[17:], loads[16], *loads[:16]]:
        load.start()
    loads[17].wait()
    rows_s[...] = back_s[...].astype(high)
    slots = asked_ref.shape[2]
    loads[18].wait()

    @pl.loop(0, rows_s.shape[0] // unroll)
    def _(group):
        base = group * unroll
        peer, first = lax.div(base, slots), lax.rem(base, slots)
        places = [pl.ds(asked_ref[peer, 0, first + k], 1) for k in range(unroll)]
        values = [
            node_s[place, :] + rows_s[pl.ds(base + k, 1), :] for k, place in enumerate(places)
        ]
        for place, value in zip(places, values):
            node_s[place, :] = value

    stores = [pltpu.make_async_copy(node_s, results[20], store_sem.at[20])]
    stores[0].start()
    for load in loads[:17]:
        load.wait()
    gradient = summed_s[...].astype(high)
    square = jnp.sum(gradient * gradient, axis=0, keepdims=True)
    grad_norm = jnp.sqrt(jnp.sum(square, axis=1, keepdims=True))
    norm_ref[0] = grad_norm[0, 0]
    factor = clip_level / jnp.maximum(grad_norm, clip_level)
    for k in range(4):
        values = [place[...] for place in loaded[4 * k : 4 * k + 4]]
        updates = adamw_step(*values, gradient[FIRST[k] : FIRST[k + 1]], factor)
        for place, value in enumerate(updates):
            place += 5 * k
            staged[place][...] = value
            store = pltpu.make_async_copy(staged[place], results[place], store_sem.at[place])
            store.start()
            stores.append(store)
    for store in stores:
        store.wait()


def finish_call(asked, part, back, summed, tensors):
    smem = pl.BlockSpec(memory_space=pltpu.SMEM)
    hbm = pl.BlockSpec(memory_space=pltpu.HBM)
    sources = [*tensors, summed, back, part]
    shapes = []
    for k in range(4):
        shape = tensors[4 * k].shape
        shapes += [jax.ShapeDtypeStruct(shape, kind) for kind in (high, high, high, low, high)]
    return pl.pallas_call(
        functools.partial(finish_kernel, 32),
        in_specs=[smem] + [hbm] * 19,
        out_specs=[smem] + [hbm] * 21,
        out_shape=[
            jax.ShapeDtypeStruct((1,), high),
            *shapes,
            jax.ShapeDtypeStruct(part.shape, high),
        ],
        scratch_shapes=[
            *[pltpu.VMEM(item.shape, item.dtype) for item in sources],
            pltpu.VMEM(back.shape, high),
            *[pltpu.VMEM(item.shape, item.dtype) for item in shapes],
            pltpu.SemaphoreType.DMA((19,)),
            pltpu.SemaphoreType.DMA((21,)),
        ],
        compiler_params=pltpu.CompilerParams(vmem_limit_bytes=VMEM),
        name="finish",
    )(asked, *sources)


def shards(
    node_in,
    edge_in,
    edge_slot,
    edge_receiver,
    edge_count,
    request,
    node_cot,
    edge_cot,
    *tensors,
):
    groups, peers = lax.axis_size("grp"), lax.axis_size("dom")
    slots = request.shape[2]
    z = Sizes(edge_in.shape[0], node_in.shape[0], peers * slots, groups * peers)
    slot_rows, asked = fetch_call(peers, request, node_in)
    node_out, edge_out, node_part, edge_grad, slot_grad, grads = layer_call(
        z,
        edge_count,
        edge_slot.reshape(-1, 128),
        edge_receiver.reshape(-1, 128),
        edge_in,
        edge_cot,
        node_in,
        node_cot,
        slot_rows.reshape(peers * slots, 128),
        tensors[::4],
    )
    summed, returned = reduce_call(groups, peers, grads, slot_grad.reshape(peers, slots, 128))
    flat = [tensor.reshape(-1, 128) for tensor in tensors]
    grad_norm, *results, node_grad = finish_call(
        asked, node_part, returned.reshape(peers * slots, 128), summed, flat
    )
    results = [value.reshape(tensors[k // 5 * 4].shape) for k, value in enumerate(results)]
    return (node_out, edge_out, node_grad, edge_grad, grad_norm.reshape(()), *results)


def solution(mesh):
    rows = P(("grp", "dom"), None)
    in_specs = (
        rows,
        rows,
        P(("grp", "dom")),
        P(("grp", "dom")),
        P(("grp", "dom")),
        P(("grp", "dom"), None, None),
        rows,
        rows,
    ) + (P(),) * 16
    out_specs = (rows,) * 4 + (P(),) * 21
    return jax.shard_map(shards, mesh=mesh, in_specs=in_specs, out_specs=out_specs, check_vma=False)
```

time: 583 us -> 114 us (0.20); the launches traced: 575 us -> 114 us
  matrix products: 250 us -> 0 us
  other arithmetic: 141 us -> 0 us
  Pallas kernels: 0 us -> 112 us
  waiting for transfers between devices: 87.7 us -> 0 us
  blocking collectives: 41 us -> 0 us
  local copies, waits for them, and re-layouts: 19.8 us -> 0 us
  between operations: 19.6 us -> 1.34 us
  starting transfers between devices: 16.1 us -> 0 us
    dot_general x32 -> x0, matrix products: 250 us -> none  [the longest x10 78 us: matmul(): return jnp.dot(operand, weights, preferred_element_type=jnp.float32)]
    pallas_call x0 -> x4, Pallas kernels: none -> 112 us  [the longest x1 55.3 us: layer_call(): pl.pallas_call(functools.partial(layer_kernel, z), grid=(z.steps,), in_sp...]
    psum x1 -> x0, waiting for transfers between devices: 79.7 us -> none  [shards(): lax.psum((grad_edge_entry, grad_node_entry, grad_inner, grad_vectors), ('...]
    reduce_sum x10 -> x0, other arithmetic: 71.2 us -> none  [the longest x1 28.2 us: shards(): grad_edge_gain = jnp.sum(message_grad * edge_normed, axis=0)]
    add x5 -> x0, other arithmetic: 43.8 us -> none  [the longest x1 35.9 us: shards(): edge_grad = edge_upstream + edge_input_grad[:, :width]]
    psum x1 -> x0, blocking collectives: 41 us -> none  [shards(): lax.psum((grad_edge_entry, grad_node_entry, grad_inner, grad_vectors), ('...]
    convert_element_type x9 -> x0, other arithmetic: 21.8 us -> none  [the longest x1 16.7 us: shards(): edge_out = (edge_in.astype(jnp.float32) + message).astype(jnp.bfloat16)]
    all_to_all x3 -> x0, starting transfers between devices: 16.1 us -> none  [the longest x1 6.33 us: shards(): lax.all_to_all(wanted, 'dom', split_axis=0, concat_axis=0, tiled=True)]
  transfers between devices with their start and end apart: 4 -> 0, of which waited for: 2 -> 0; matrix products, arithmetic and copies ran while one was open for 11% -> 0% of each run, Pallas kernels for 0% -> 0%
where the time goes in v1:
time: 114 us
  Pallas kernels  112 us (98%)
  between operations  1.34 us (1%)
    pallas_call x1, Pallas kernels, layer_call(): pl.pallas_call(functools.partial(layer_kernel, z), grid=(z.steps,), in_sp...  55.3 us
    pallas_call x1, Pallas kernels, reduce_call(): pl.pallas_call(functools.partial(reduce_kernel, groups, peers), in_specs=...  23.2 us
    pallas_call x1, Pallas kernels, fetch_call(): pl.pallas_call(functools.partial(fetch_kernel, peers, 32), in_specs=[hbm,...  21.7 us
    pallas_call x1, Pallas kernels, finish_call(): pl.pallas_call(functools.partial(finish_kernel, 32), in_specs=[smem] + [h...  12.2 us

profile of v1, /device:TPU:0, one launch (start us, length us, event | category | flops | bytes accessed | tf_op | source)
XLA Modules:
  0.0 113.7 jit_solution(9490018822239994868)
XLA Ops:
  1.3 21.7 %fetch.1 = (bf16[8,256,128]{2,1,0:T(8,128)(2,1)}, s32[8,1,256]{2,1,0:T(1,128)}) custom-call(s32[8,256]{1,0:T(8,128)} %bitcast.25, bf16[4096,128]{1,0:T(8,128)(2,1)} %node_in_ref.1), custom_call_target="tpu_custom_call" | custom-call | tf_op jit(solution)/shard_map/fetch/pallas_call | solution.py:594
  23.0 55.3 %layer.1 = (bf16[4096,128]{1,0:T(8,128)(2,1)}, bf16[32768,128]{1,0:T(8,128)(2,1)}, f32[4096,128]{1,0:T(8,128)}, f32[32768,128]{1,0:T(8,128)}, bf16[2048,128]{1,0:T(8,128)(2,1)}, /*index=5*/f32[1536,128]{1,0:T(8,128)}) custom-call(s32[1]{0:T(128)S(6)} %copy.49.count_ref, s32[256,128]{1,0:T(8,128)} %bitcast.23, s32[256,128]{1,0:T(8,128)} %bitcast.24, ...), custom_call_target="tpu_custom_call" | custom-call | tf_op jit(solution)/shard_map/layer/pallas_call | solution.py:433
  78.4 23.2 %reduce.1 = (bf16[1536,128]{1,0:T(8,128)(2,1)}, bf16[8,256,128]{2,1,0:T(8,128)(2,1)}) custom-call(f32[1536,128]{1,0:T(8,128)} %get-tuple-element.61.grads_ref, bf16[8,256,128]{2,1,0:T(8,128)(2,1)} %bitcast.18), custom_call_target="tpu_custom_call" | custom-call | tf_op jit(solution)/shard_map/reduce/pallas_call | solution.py:773
  101.5 12.2 %finish.1 = (f32[1]{0:T(128)}, f32[384,128]{1,0:T(8,128)}, f32[384,128]{1,0:T(8,128)}, f32[384,128]{1,0:T(8,128)}, bf16[384,128]{1,0:T(8,128)(2,1)}, /*index=5*/...) custom-call(s32[8,1,256]{2,1,0:T(1,128)} %get-tuple-element.60.asked, ...), custom_call_target="tpu_custom_call" | custom-call | tf_op jit(solution)/shard_map/finish/pallas_call | solution.py:889

commit v2 on v1

--- a/solution.py
+++ b/solution.py
@@ -265,13 +265,11 @@
         slope_two_s[wide_rows, :] = slope
         yield
         center = dot(act_two, wide_s[1]) + twice(bias_three)
-        square = (center * center).astype(low)
-        yield
-        inverse = lax.rsqrt(dot(square, wide_s[5]) + eps_norm)
         yield
         messages = []
-        for index, center, inverse in zip(indices, sides(center), sides(inverse)):
+        for index, center in zip(indices, sides(center)):
             live = live_rows(index)
+            inverse = lax.rsqrt(jnp.mean(center * center, axis=1, keepdims=True) + eps_norm)
             inverse = jnp.where(live, inverse, 0.0)
             normed = center * inverse
             normed_s[chunk_rows(index), :] = normed
@@ -343,7 +341,7 @@
     def edge_backward(pair):
         wide_rows = chunk_rows(pair)
         indices = (2 * pair, 2 * pair + 1)
-        upstreams, plains, crosses = [], [], []
+        upstreams, plains = [], []
         for index in indices:
             tables = [
                 jnp.zeros((cs, 256), low),
@@ -359,17 +357,13 @@
             upstreams.append(upstream)
             plains.append(plain)
             yield
-        for index, upstream in zip(indices, upstreams):
-            cross = upstream * normed_s[chunk_rows(index), :]
+        threes = []
+        for index, upstream, plain in zip(indices, upstreams, plains):
+            normed = normed_s[chunk_rows(index), :]
+            cross = upstream * normed
             sums_s[3] += fold_rows(cross)
             sums_s[4] += fold_rows(jnp.where(live_rows(index), upstream, 0.0))
-            crosses.append(cross.astype(low))
-        yield
-        means = dot(jnp.concatenate(crosses, axis=1), wide_s[6])
-        yield
-        threes = []
-        for index, upstream, plain, cross in zip(indices, upstreams, plains, sides(means)):
-            normed = normed_s[chunk_rows(index), :]
+            cross = jnp.mean(cross * vec[3], axis=1, keepdims=True)
             d_three = inverse_s[chunk_rows(index), :] * (
                 upstream * vec[3] - plain - normed * cross
             )

time: 114 us -> 114 us (level)
  no operation moved by 1% of the time
where the time goes in v2:
time: 114 us; the launch traced here: 113 us
  Pallas kernels  112 us (98%)
  between operations  1.34 us (1%)
    pallas_call x1, Pallas kernels, layer_call(): pl.pallas_call(functools.partial(layer_kernel, z), grid=(z.steps,), in_sp...  54.9 us
    pallas_call x1, Pallas kernels, reduce_call(): pl.pallas_call(functools.partial(reduce_kernel, groups, peers), in_specs=...  23.2 us
    pallas_call x1, Pallas kernels, fetch_call(): pl.pallas_call(functools.partial(fetch_kernel, peers, 32), in_specs=[hbm,...  21.7 us
    pallas_call x1, Pallas kernels, finish_call(): pl.pallas_call(functools.partial(finish_kernel, 32), in_specs=[smem] + [h...  12.2 us

profile of v2, /device:TPU:0, one launch (start us, length us, event | category | flops | bytes accessed | tf_op | source)
XLA Modules:
  0.0 113.3 jit_solution(3177956378516536012)
XLA Ops:
  1.3 21.7 %fetch.1 = (bf16[8,256,128]{2,1,0:T(8,128)(2,1)}, s32[8,1,256]{2,1,0:T(1,128)}) custom-call(s32[8,256]{1,0:T(8,128)} %bitcast.25, bf16[4096,128]{1,0:T(8,128)(2,1)} %node_in_ref.1), custom_call_target="tpu_custom_call" | custom-call | tf_op jit(solution)/shard_map/fetch/pallas_call | solution.py:588
  23.0 54.9 %layer.1 = (bf16[4096,128]{1,0:T(8,128)(2,1)}, bf16[32768,128]{1,0:T(8,128)(2,1)}, f32[4096,128]{1,0:T(8,128)}, f32[32768,128]{1,0:T(8,128)}, bf16[2048,128]{1,0:T(8,128)(2,1)}, /*index=5*/f32[1536,128]{1,0:T(8,128)}) custom-call(s32[1]{0:T(128)S(6)} %copy.49.count_ref, s32[256,128]{1,0:T(8,128)} %bitcast.23, s32[256,128]{1,0:T(8,128)} %bitcast.24, ...), custom_call_target="tpu_custom_call" | custom-call | tf_op jit(solution)/shard_map/layer/pallas_call | solution.py:427
  77.9 23.2 %reduce.1 = (bf16[1536,128]{1,0:T(8,128)(2,1)}, bf16[8,256,128]{2,1,0:T(8,128)(2,1)}) custom-call(f32[1536,128]{1,0:T(8,128)} %get-tuple-element.61.grads_ref, bf16[8,256,128]{2,1,0:T(8,128)(2,1)} %bitcast.18), custom_call_target="tpu_custom_call" | custom-call | tf_op jit(solution)/shard_map/reduce/pallas_call | solution.py:767
  101.1 12.2 %finish.1 = (f32[1]{0:T(128)}, f32[384,128]{1,0:T(8,128)}, f32[384,128]{1,0:T(8,128)}, f32[384,128]{1,0:T(8,128)}, bf16[384,128]{1,0:T(8,128)(2,1)}, /*index=5*/...) custom-call(s32[8,1,256]{2,1,0:T(1,128)} %get-tuple-element.60.asked, ...), custom_call_target="tpu_custom_call" | custom-call | tf_op jit(solution)/shard_map/finish/pallas_call | solution.py:883

commit v3 on v2

--- a/solution.py
+++ b/solution.py
@@ -25,9 +25,11 @@
 low = jnp.bfloat16
 high = jnp.float32
 
-GAP = 4
+GAP = 2
+PIECE = 64
+PIECE_NORM = 32
 VMEM = 60 * 1024 * 1024
-PAIRS = 8
+PAIRS = 2
 
 
 def dot(operand, weights):
@@ -102,8 +104,8 @@
         self.chunk_slots = self.sub * self.swin
         self.chunk_nodes = self.sub * self.rwin
         self.pair_nodes, self.pair_slots = 2 * self.chunk_nodes, 2 * self.chunk_slots
-        self.per_group = 4
-        self.pairs = PAIRS
+        self.per_group = 2
+        self.pairs = max(PAIRS, 1024 // (2 * self.chunk))
         self.group_nodes = self.per_group * self.pair_nodes
         self.group_slots = self.per_group * self.pair_slots
         self.tile = self.pairs * 2 * self.chunk
@@ -158,6 +160,10 @@
     slope_two_s,
     normed_s,
     inverse_s,
+    message_s,
+    node_act_s,
+    node_slope_s,
+    node_back_s,
     gathered_s,
     table_s,
     slot_pre_s,
@@ -200,12 +206,12 @@
     w_edge, w_slot, w_recv = edge_low[:128], edge_low[128:256], edge_low[256:]
     bias_three = vec[2] - jnp.mean(vec[2], axis=1, keepdims=True)
     gain_part = below_s[:, 128:]
-    row_ids = lax.broadcasted_iota(jnp.int32, (chunk, 128), 0)
     slot_pre_s[...] = dot(slot_ref[...], w_slot).astype(low)
     node_pre_s[...] = (dot(node_in_ref[...], w_recv) + vec[0]).astype(low)
 
-    def live_rows(index):
-        return row_ids < count_ref[0] - (step * z.tile + index * chunk)
+    def live_rows(index, first, count):
+        rows = lax.broadcasted_iota(jnp.int32, (count, 128), 0)
+        return rows < count_ref[0] - (step * z.tile + index * chunk + first)
 
     def sides(wide):
         return wide[:, :128], wide[:, 128:]
@@ -213,35 +219,45 @@
     def chunk_rows(index):
         return pl.ds(index * chunk, chunk)
 
-    def hot_columns(index):
-        columns = []
-        for k in range(z.sub):
-            block = index * z.sub + k
-            number = step * (z.tile // 128) + block
-            pieces = []
-            for ref, width, count in ((slot_ids_ref, z.swin, cs), (recv_ids_ref, z.rwin, cn)):
-                ids = ref[pl.ds(block, 1), :] - number * width
-                band = lax.broadcasted_iota(jnp.int32, (width, 128), 0) == ids
-                above, below = k * width, count - (k + 1) * width
-                if above:
-                    pieces.append(jnp.zeros((above, 128), high))
-                pieces.append(jnp.where(band, 1.0, 0.0))
-                if below:
-                    pieces.append(jnp.zeros((below, 128), high))
-            if pad:
-                pieces.append(jnp.zeros((pad, 128), high))
-            columns.append(jnp.concatenate(pieces, axis=0).astype(low))
-        return jnp.concatenate(columns, axis=1)
+    def hot_block(block, k):
+        pieces = []
+        number = step * (z.tile // 128) + block
+        for ref, width, count in ((slot_ids_ref, z.swin, cs), (recv_ids_ref, z.rwin, cn)):
+            ids = ref[pl.ds(block, 1), :] - number * width
+            band = lax.broadcasted_iota(jnp.int32, (width, 128), 0) == ids
+            above, below = k * width, count - (k + 1) * width
+            if above:
+                pieces.append(jnp.zeros((above, 128), high))
+            pieces.append(jnp.where(band, 1.0, 0.0))
+            if below:
+                pieces.append(jnp.zeros((below, 128), high))
+        if pad:
+            pieces.append(jnp.zeros((pad, 128), high))
+        return jnp.concatenate(pieces, axis=0).astype(low)
+
+    def row_pieces(count, rows):
+        rows = min(count, rows)
+        return [(first, first + rows) for first in range(0, count, rows)]
+
+    def gelu_rows(pre, act_s, slope_s, base):
+        for first, last in row_pieces(pre.shape[0], PIECE):
+            act, slope = gelu_pair(pre[first:last].astype(low))
+            act_s[pl.ds(base + first, last - first), :] = act
+            slope_s[pl.ds(base + first, last - first), :] = slope
 
     def edge_forward(pair):
+        base = pair * chunk
         wide_rows = chunk_rows(pair)
         indices = (2 * pair, 2 * pair + 1)
+        for index in indices:
+            for k in range(z.sub):
+                block = index * z.sub + k
+                hot_t = hot_block(block, k)
+                pick_t[index, :, k * 128 : (k + 1) * 128] = hot_t
+                pick_s[pl.ds(block * 128, 128), :] = hot_t.T
+        yield
         pres = []
-        for side, index in enumerate(indices):
-            hot_t = hot_columns(index)
-            hot = hot_t.T
-            pick_t[index] = hot_t
-            pick_s[chunk_rows(index), :] = hot
+        for index in indices:
             tables = [
                 w_edge,
                 slot_pre_s[pl.ds(index * cs, cs), :],
@@ -249,100 +265,117 @@
             ]
             if pad:
                 tables.append(jnp.zeros((pad, 128), low))
-            rows = edge_in_ref[chunk_rows(index), :]
-            pres.append(
-                dot(jnp.concatenate([rows, hot], axis=1), jnp.concatenate(tables, axis=0)).astype(low)
+            entry = jnp.concatenate(
+                [edge_in_ref[chunk_rows(index), :], pick_s[chunk_rows(index), :]], axis=1
             )
+            pres.append(dot(entry, jnp.concatenate(tables, axis=0)))
+        yield
+        gelu_rows(jnp.concatenate(pres, axis=1), act_one_s, slope_one_s, base)
+        yield
+        pre_two = dot(act_one_s[wide_rows, :], wide_s[0])
+        yield
+        bias = twice(vec[1])
+        for first, last in row_pieces(chunk, PIECE):
+            act, slope = gelu_pair((pre_two[first:last] + bias).astype(low))
+            act_two_s[pl.ds(base + first, last - first), :] = act
+            slope_two_s[pl.ds(base + first, last - first), :] = slope
+        yield
+        pre_three = dot(act_two_s[wide_rows, :], wide_s[1])
+        yield
+        for side, index in enumerate(indices):
+            half = pre_three[:, side * 128 : (side + 1) * 128]
+            for first, last in row_pieces(chunk, PIECE_NORM):
+                rows = pl.ds(index * chunk + first, last - first)
+                live = live_rows(index, first, last - first)
+                center = half[first:last] + bias_three
+                inverse = lax.rsqrt(jnp.mean(center * center, axis=1, keepdims=True) + eps_norm)
+                inverse = jnp.where(live, inverse, 0.0)
+                normed = center * inverse
+                normed_s[rows, :] = normed
+                inverse_s[rows, :] = inverse
+                message = jnp.where(live, normed * vec[3] + vec[4], 0.0)
+                edge_out_ref[rows, :] = (edge_in_ref[rows, :].astype(high) + message).astype(low)
+                message_s[
+                    pl.ds(base + first, last - first), side * 128 : (side + 1) * 128
+                ] = message.astype(low)
             yield
-        act_one, slope = gelu_pair(jnp.concatenate(pres, axis=1))
-        act_one_s[wide_rows, :] = act_one
-        slope_one_s[wide_rows, :] = slope
-        yield
-        pre_two = (dot(act_one, wide_s[0]) + twice(vec[1])).astype(low)
-        yield
-        act_two, slope = gelu_pair(pre_two)
-        act_two_s[wide_rows, :] = act_two
-        slope_two_s[wide_rows, :] = slope
-        yield
-        center = dot(act_two, wide_s[1]) + twice(bias_three)
-        yield
-        messages = []
-        for index, center in zip(indices, sides(center)):
-            live = live_rows(index)
-            inverse = lax.rsqrt(jnp.mean(center * center, axis=1, keepdims=True) + eps_norm)
-            inverse = jnp.where(live, inverse, 0.0)
-            normed = center * inverse
-            normed_s[chunk_rows(index), :] = normed
-            inverse_s[chunk_rows(index), :] = inverse
-            message = jnp.where(live, normed * vec[3] + vec[4], 0.0)
-            rows = edge_in_ref[chunk_rows(index), :]
-            edge_out_ref[chunk_rows(index), :] = (rows.astype(high) + message).astype(low)
-            messages.append(message.astype(low))
-        yield
         hots = [pick_t[index, cs : cs + cn, :] for index in indices]
-        total = dot(jnp.concatenate(hots, axis=0), jnp.concatenate(messages, axis=1)).astype(low)
+        total = dot(jnp.concatenate(hots, axis=0), message_s[wide_rows, :]).astype(low)
         gathered_s[pl.ds(indices[0] * cn, cn), :] = total[:cn, :128]
         gathered_s[pl.ds(indices[1] * cn, cn), :] = total[cn:, 128:]
         yield
 
     def node_phase(group):
-        rows = pl.ds(group * z.group_nodes, z.group_nodes)
-        node_rows = node_in_ref[rows, :]
-        entry = jnp.concatenate([node_rows, gathered_s[rows, :]], axis=1)
-        node_one = (dot(entry, node_low) + vec[5]).astype(low)
-        yield
-        act_one, slope_one = gelu_pair(node_one)
-        yield
-        node_two = (dot(act_one, inner_low[2]) + vec[6]).astype(low)
-        yield
-        act_two, slope_two = gelu_pair(node_two)
-        yield
-        node_three = dot(act_two, inner_low[3]) + vec[7]
-        yield
-        center = node_three - jnp.mean(node_three, axis=1, keepdims=True)
-        inverse = lax.rsqrt(jnp.mean(center * center, axis=1, keepdims=True) + eps_norm)
-        normed = center * inverse
-        node_out_ref[rows, :] = (node_rows.astype(high) + normed * vec[8] + vec[9]).astype(low)
-        yield
-        upstream = node_cot_ref[rows, :].astype(high)
-        sums_s[8] += fold_rows(upstream * normed)
-        sums_s[9] += fold_rows(upstream)
-        upper = upstream * vec[8]
-        mean_plain = jnp.mean(upper, axis=1, keepdims=True)
-        mean_cross = jnp.mean(upper * normed, axis=1, keepdims=True)
-        d_three = inverse * (upper - mean_plain - normed * mean_cross)
-        sums_s[7] += fold_rows(d_three)
-        d_three = d_three.astype(low)
-        yield
-        back = dot_nt(d_three, inner_low[3])
-        yield
-        d_two = back * slope_two.astype(high)
-        sums_s[6] += fold_rows(d_two)
-        d_two = d_two.astype(low)
-        yield
-        back = dot_nt(d_two, inner_low[2])
-        yield
-        d_one = back * slope_one.astype(high)
-        sums_s[5] += fold_rows(d_one)
-        d_one = d_one.astype(low)
-        yield
-        back = dot_nt(d_one, node_low)
-        node_grad_ref[rows, :] = upstream + back[:, :128]
-        arrived = back[:, 128:].astype(low)
-        yield
-        table_s[rows, :128] = arrived
-        table_s[rows, 128:] = dot(arrived, gain_part).astype(low)
-        yield
-        grads_ref[384:640, :] += dot_tn(entry, d_one)
-        grads_ref[896:1024, :] += dot_tn(act_one, d_two)
-        grads_ref[1024:1152, :] += dot_tn(act_two, d_three)
+        base = group * z.group_nodes
+        rows = pl.ds(base, z.group_nodes)
+        parts = row_pieces(z.group_nodes, PIECE)
+
+        def here(first, last):
+            return pl.ds(base + first, last - first)
+
+        entry = jnp.concatenate([node_in_ref[rows, :], gathered_s[rows, :]], axis=1)
+        pre = dot(entry, node_low)
+        yield
+        for first, last in parts:
+            act, slope = gelu_pair((pre[first:last] + vec[5]).astype(low))
+            node_act_s[0, here(first, last), :] = act
+            node_slope_s[0, here(first, last), :] = slope
+        yield
+        pre = dot(node_act_s[0, rows, :], inner_low[2])
+        yield
+        for first, last in parts:
+            act, slope = gelu_pair((pre[first:last] + vec[6]).astype(low))
+            node_act_s[1, here(first, last), :] = act
+            node_slope_s[1, here(first, last), :] = slope
+        yield
+        pre = dot(node_act_s[1, rows, :], inner_low[3])
+        yield
+        for first, last in parts:
+            piece = here(first, last)
+            value = pre[first:last] + vec[7]
+            center = value - jnp.mean(value, axis=1, keepdims=True)
+            inverse = lax.rsqrt(jnp.mean(center * center, axis=1, keepdims=True) + eps_norm)
+            normed = center * inverse
+            node_out_ref[piece, :] = (
+                node_in_ref[piece, :].astype(high) + normed * vec[8] + vec[9]
+            ).astype(low)
+            upstream = node_cot_ref[piece, :].astype(high)
+            sums_s[8] += fold_rows(upstream * normed)
+            sums_s[9] += fold_rows(upstream)
+            upper = upstream * vec[8]
+            mean_plain = jnp.mean(upper, axis=1, keepdims=True)
+            mean_cross = jnp.mean(upper * normed, axis=1, keepdims=True)
+            d_three = inverse * (upper - mean_plain - normed * mean_cross)
+            sums_s[7] += fold_rows(d_three)
+            node_back_s[2, piece, :] = d_three.astype(low)
+        yield
+        for k in (1, 0):
+            back = dot_nt(node_back_s[k + 1, rows, :], inner_low[2 + k])
+            yield
+            for first, last in parts:
+                piece = here(first, last)
+                value = back[first:last] * node_slope_s[k, piece, :].astype(high)
+                sums_s[5 + k] += fold_rows(value)
+                node_back_s[k, piece, :] = value.astype(low)
+            yield
+        back = dot_nt(node_back_s[0, rows, :], node_low)
+        for first, last in parts:
+            piece = here(first, last)
+            node_grad_ref[piece, :] = node_cot_ref[piece, :].astype(high) + back[first:last, :128]
+            table_s[piece, :128] = back[first:last, 128:].astype(low)
+        yield
+        table_s[rows, 128:] = dot(table_s[rows, :128], gain_part).astype(low)
+        yield
+        grads_ref[384:640, :] += dot_tn(entry, node_back_s[0, rows, :])
+        grads_ref[896:1024, :] += dot_tn(node_act_s[0, rows, :], node_back_s[1, rows, :])
+        grads_ref[1024:1152, :] += dot_tn(node_act_s[1, rows, :], node_back_s[2, rows, :])
         yield
 
     def edge_backward(pair):
+        base = pair * chunk
         wide_rows = chunk_rows(pair)
         indices = (2 * pair, 2 * pair + 1)
-        upstreams, plains = [], []
-        for index in indices:
+        for side, index in enumerate(indices):
             tables = [
                 jnp.zeros((cs, 256), low),
                 table_s[pl.ds(index * cn, cn), :],
@@ -353,40 +386,47 @@
             entry = jnp.concatenate(
                 [pick_s[chunk_rows(index), :], edge_cot_ref[chunk_rows(index), :]], axis=1
             )
-            upstream, plain = sides(dot(entry, jnp.concatenate(tables, axis=0)))
-            upstreams.append(upstream)
-            plains.append(plain)
+            arrived = dot(entry, jnp.concatenate(tables, axis=0))
             yield
-        threes = []
-        for index, upstream, plain in zip(indices, upstreams, plains):
-            normed = normed_s[chunk_rows(index), :]
-            cross = upstream * normed
-            sums_s[3] += fold_rows(cross)
-            sums_s[4] += fold_rows(jnp.where(live_rows(index), upstream, 0.0))
-            cross = jnp.mean(cross * vec[3], axis=1, keepdims=True)
-            d_three = inverse_s[chunk_rows(index), :] * (
-                upstream * vec[3] - plain - normed * cross
-            )
-            threes.append(d_three.astype(low))
-        d_three = jnp.concatenate(threes, axis=1)
-        yield
-        d_two = dot(d_three, wide_s[3]).astype(low) * slope_two_s[wide_rows, :]
-        yield
-        d_one = dot(d_two, wide_s[2]).astype(low) * slope_one_s[wide_rows, :]
-        yield
-        for index, back in zip(indices, sides(dot(d_one, wide_s[4]))):
-            edge_grad_ref[chunk_rows(index), :] = (
-                edge_cot_ref[chunk_rows(index), :].astype(high) + back
-            )
+            gain_sum = jnp.zeros((8, 128), high)
+            shift_sum = jnp.zeros((8, 128), high)
+            for first, last in row_pieces(chunk, PIECE_NORM):
+                rows = pl.ds(index * chunk + first, last - first)
+                upstream, plain = sides(arrived[first:last])
+                normed = normed_s[rows, :]
+                cross = upstream * normed
+                gain_sum = gain_sum + fold_rows(cross)
+                live = live_rows(index, first, last - first)
+                shift_sum = shift_sum + fold_rows(jnp.where(live, upstream, 0.0))
+                cross = jnp.mean(cross * vec[3], axis=1, keepdims=True)
+                d_three = inverse_s[rows, :] * (upstream * vec[3] - plain - normed * cross)
+                message_s[
+                    pl.ds(base + first, last - first), side * 128 : (side + 1) * 128
+                ] = d_three.astype(low)
+            sums_s[3] += gain_sum
+            sums_s[4] += shift_sum
+            yield
+        for gradient_s, slope_s, weights in ((message_s, slope_two_s, 3), (slope_two_s, slope_one_s, 2)):
+            back = dot(gradient_s[wide_rows, :], wide_s[weights])
+            yield
+            for first, last in row_pieces(chunk, PIECE):
+                rows = pl.ds(base + first, last - first)
+                slope_s[rows, :] = back[first:last].astype(low) * slope_s[rows, :]
+            yield
+        back = dot(slope_one_s[wide_rows, :], wide_s[4])
+        yield
+        for index, half in zip(indices, sides(back)):
+            for first, last in row_pieces(chunk, PIECE):
+                rows = pl.ds(index * chunk + first, last - first)
+                edge_grad_ref[rows, :] = edge_cot_ref[rows, :].astype(high) + half[first:last]
         yield
         ones = jnp.ones((16, chunk), low)
         entry = [edge_in_ref[chunk_rows(index), :].T for index in indices]
         hots = [pick_t[index, : cs + cn, :] for index in indices]
-        total = dot(jnp.concatenate(entry + hots, axis=0), d_one)
+        total = dot(jnp.concatenate(entry + hots, axis=0), slope_one_s[wide_rows, :])
         grads_ref[0:128, :] += total[:128, :128] + total[128:256, 128:]
         first = total[256 : 256 + cs + cn, :128]
         second = total[256 + cs + cn :, 128:]
-        yield
         node_rows = pl.ds(pair * z.pair_nodes, z.pair_nodes)
         slot_rows = pl.ds(pair * z.pair_slots, z.pair_slots)
         slot_sum_s[slot_rows, :] = jnp.concatenate([first[:cs], second[:cs]], axis=0).astype(low)
@@ -394,8 +434,10 @@
         sums_s[0] += fold_rows(recv_sum)
         recv_sum_s[node_rows, :] = recv_sum.astype(low)
         yield
-        for k, act_s, gradient in ((1, act_one_s, d_two), (2, act_two_s, d_three)):
-            total = dot(jnp.concatenate([act_s[wide_rows, :].T, ones], axis=0), gradient)
+        for k, act_s, gradient_s in ((1, act_one_s, slope_two_s), (2, act_two_s, message_s)):
+            total = dot(
+                jnp.concatenate([act_s[wide_rows, :].T, ones], axis=0), gradient_s[wide_rows, :]
+            )
             grads_ref[pl.ds(512 + 128 * k, 128), :] += total[:128, :128] + total[128:256, 128:]
             sums_s[k] += (total[256:264, :128] + total[256:264, 128:]) * 0.125
             yield
@@ -463,6 +505,10 @@
             pltpu.VMEM((z.tile // 2, 256), low),
             pltpu.VMEM((z.tile, 128), high),
             pltpu.VMEM((z.tile, 128), high),
+            pltpu.VMEM((z.tile // 2, 256), low),
+            pltpu.VMEM((2, z.tile_nodes, 128), low),
+            pltpu.VMEM((2, z.tile_nodes, 128), low),
+            pltpu.VMEM((3, z.tile_nodes, 128), low),
             pltpu.VMEM((z.tile_nodes, 128), low),
             pltpu.VMEM((z.tile_nodes, 256), low),
             pltpu.VMEM((z.tile_slots, 128), low),

time: 114 us -> 137 us (1.20)
  Pallas kernels: 112 us -> 135 us
    pallas_call x1, Pallas kernels: 54.9 us -> 78.3 us  [layer_call(): pl.pallas_call(functools.partial(layer_kernel, z), grid=(z.steps,), in_sp...]
where the time goes in v3:
time: 137 us
  Pallas kernels  135 us (99%)
    pallas_call x1, Pallas kernels, layer_call(): pl.pallas_call(functools.partial(layer_kernel, z), grid=(z.steps,), in_sp...  78.3 us
    pallas_call x1, Pallas kernels, reduce_call(): pl.pallas_call(functools.partial(reduce_kernel, groups, peers), in_specs=...  23.1 us
    pallas_call x1, Pallas kernels, fetch_call(): pl.pallas_call(functools.partial(fetch_kernel, peers, 32), in_specs=[hbm,...  21.7 us
    pallas_call x1, Pallas kernels, finish_call(): pl.pallas_call(functools.partial(finish_kernel, 32), in_specs=[smem] + [h...  12.2 us

profile of v3, /device:TPU:0, one launch (start us, length us, event | category | flops | bytes accessed | tf_op | source)
XLA Modules:
  0.0 136.7 jit_solution(12121577281848165582)
XLA Ops:
  1.3 21.7 %fetch.1 = (bf16[8,256,128]{2,1,0:T(8,128)(2,1)}, s32[8,1,256]{2,1,0:T(1,128)}) custom-call(s32[8,256]{1,0:T(8,128)} %bitcast.25, bf16[4096,128]{1,0:T(8,128)(2,1)} %node_in_ref.1), custom_call_target="tpu_custom_call" | custom-call | tf_op jit(solution)/shard_map/fetch/pallas_call | solution.py:634
  23.0 78.3 %layer.1 = (bf16[4096,128]{1,0:T(8,128)(2,1)}, bf16[32768,128]{1,0:T(8,128)(2,1)}, f32[4096,128]{1,0:T(8,128)}, f32[32768,128]{1,0:T(8,128)}, bf16[2048,128]{1,0:T(8,128)(2,1)}, /*index=5*/f32[1536,128]{1,0:T(8,128)}) custom-call(s32[1]{0:T(128)S(6)} %copy.49.count_ref, s32[256,128]{1,0:T(8,128)} %bitcast.23, s32[256,128]{1,0:T(8,128)} %bitcast.24, ...), custom_call_target="tpu_custom_call" | custom-call | tf_op jit(solution)/shard_map/layer/pallas_call | solution.py:469
  101.4 23.1 %reduce.1 = (bf16[1536,128]{1,0:T(8,128)(2,1)}, bf16[8,256,128]{2,1,0:T(8,128)(2,1)}) custom-call(f32[1536,128]{1,0:T(8,128)} %get-tuple-element.61.grads_ref, bf16[8,256,128]{2,1,0:T(8,128)(2,1)} %bitcast.18), custom_call_target="tpu_custom_call" | custom-call | tf_op jit(solution)/shard_map/reduce/pallas_call | solution.py:813
  124.5 12.2 %finish.1 = (f32[1]{0:T(128)}, f32[384,128]{1,0:T(8,128)}, f32[384,128]{1,0:T(8,128)}, f32[384,128]{1,0:T(8,128)}, bf16[384,128]{1,0:T(8,128)(2,1)}, /*index=5*/...) custom-call(s32[8,1,256]{2,1,0:T(1,128)} %get-tuple-element.60.asked, ...), custom_call_target="tpu_custom_call" | custom-call | tf_op jit(solution)/shard_map/finish/pallas_call | solution.py:929

commit v4 on v3

--- a/solution.py
+++ b/solution.py
@@ -29,7 +29,7 @@
 PIECE = 64
 PIECE_NORM = 32
 VMEM = 60 * 1024 * 1024
-PAIRS = 2
+PAIRS = 8
 
 
 def dot(operand, weights):
@@ -104,15 +104,15 @@
         self.chunk_slots = self.sub * self.swin
         self.chunk_nodes = self.sub * self.rwin
         self.pair_nodes, self.pair_slots = 2 * self.chunk_nodes, 2 * self.chunk_slots
-        self.per_group = 2
-        self.pairs = max(PAIRS, 1024 // (2 * self.chunk))
+        self.per_group = 4
+        self.pairs = PAIRS
         self.group_nodes = self.per_group * self.pair_nodes
         self.group_slots = self.per_group * self.pair_slots
         self.tile = self.pairs * 2 * self.chunk
         self.tile_chunks = 2 * self.pairs
         self.tile_nodes = self.pairs * self.pair_nodes
         self.tile_slots = self.pairs * self.pair_slots
-        self.steps = edges // self.tile
+        self.tiles = edges // self.tile
         self.grad_rows = -(-1162 // (16 * devices)) * 16 * devices
 
 
@@ -132,8 +132,30 @@
     return jnp.concatenate([row, row], axis=1)
 
 
-def layer_kernel(
+def prepare(edge_entry_ref, inner_ref, vec_ref, sums_s, wide_s, below_s):
+    sums_s[...] = jnp.zeros_like(sums_s)
+    first, second = inner_ref[0].astype(low), inner_ref[1].astype(low)
+    wide_s[0] = diagonal(first, first)
+    middle = second.astype(high)
+    middle = (middle - jnp.mean(middle, axis=1, keepdims=True)).astype(low)
+    wide_s[1] = diagonal(middle, middle)
+    for k, weights in ((2, inner_ref[0]), (3, inner_ref[1]), (4, edge_entry_ref[0:128, :])):
+        weights = weights.T.astype(low)
+        wide_s[k] = diagonal(weights, weights)
+    row = lax.broadcasted_iota(jnp.int32, (128, 128), 0)
+    column = lax.broadcasted_iota(jnp.int32, (128, 128), 1)
+    gain = jnp.broadcast_to(vec_ref[pl.ds(3, 1), :] * (1.0 / 128.0), (128, 128)).T.astype(low)
+    below_s[:, :128] = jnp.where(row == column, 1.0, 0.0).astype(low)
+    below_s[:, 128:] = gain
+
+
+def close_sums(grads_ref, sums_s):
+    grads_ref[1152:1162, :] += jnp.sum(sums_s[...], axis=1)
+
+
+def layer_tile(
     z,
+    tile,
     count_ref,
     slot_ids_ref,
     recv_ids_ref,
@@ -152,6 +174,9 @@
     edge_grad_ref,
     slot_grad_ref,
     grads_ref,
+    sums_s,
+    wide_s,
+    below_s,
     pick_s,
     pick_t,
     act_one_s,
@@ -170,36 +195,10 @@
     node_pre_s,
     slot_sum_s,
     recv_sum_s,
-    sums_s,
-    wide_s,
-    below_s,
 ):
-    step = pl.program_id(0)
     chunk, cn, cs = z.chunk, z.chunk_nodes, z.chunk_slots
     pad = 128 - cn - cs
     vec = [vec_ref[pl.ds(k, 1), :] for k in range(10)]
-
-    @pl.when(step == 0)
-    def _():
-        grads_ref[...] = jnp.zeros_like(grads_ref)
-        sums_s[...] = jnp.zeros_like(sums_s)
-        first, second = inner_ref[0].astype(low), inner_ref[1].astype(low)
-        wide_s[0] = diagonal(first, first)
-        middle = second.astype(high)
-        middle = (middle - jnp.mean(middle, axis=1, keepdims=True)).astype(low)
-        wide_s[1] = diagonal(middle, middle)
-        for k, weights in ((2, inner_ref[0]), (3, inner_ref[1]), (4, edge_entry_ref[0:128, :])):
-            weights = weights.T.astype(low)
-            wide_s[k] = diagonal(weights, weights)
-        part = jnp.full((128, 128), 1.0 / 128.0, low)
-        wide_s[5] = diagonal(part, part)
-        row = lax.broadcasted_iota(jnp.int32, (128, 128), 0)
-        column = lax.broadcasted_iota(jnp.int32, (128, 128), 1)
-        gain = jnp.broadcast_to(vec[3] * (1.0 / 128.0), (128, 128)).T.astype(low)
-        wide_s[6] = diagonal(gain, gain)
-        below_s[:, :128] = jnp.where(row == column, 1.0, 0.0).astype(low)
-        below_s[:, 128:] = gain
-
     edge_low = edge_entry_ref[...].astype(low)
     node_low = node_entry_ref[...].astype(low)
     inner_low = [None, None, inner_ref[2].astype(low), inner_ref[3].astype(low)]
@@ -211,7 +210,7 @@
 
     def live_rows(index, first, count):
         rows = lax.broadcasted_iota(jnp.int32, (count, 128), 0)
-        return rows < count_ref[0] - (step * z.tile + index * chunk + first)
+        return rows < count_ref[0] - (tile * z.tile + index * chunk + first)
 
     def sides(wide):
         return wide[:, :128], wide[:, 128:]
@@ -221,7 +220,7 @@
 
     def hot_block(block, k):
         pieces = []
-        number = step * (z.tile // 128) + block
+        number = tile * (z.tile // 128) + block
         for ref, width, count in ((slot_ids_ref, z.swin, cs), (recv_ids_ref, z.rwin, cn)):
             ids = ref[pl.ds(block, 1), :] - number * width
             band = lax.broadcasted_iota(jnp.int32, (width, 128), 0) == ids
@@ -454,76 +453,139 @@
 
     emit(z.pairs, z.per_group, edge_forward, node_phase, edge_backward, group_end)
 
-    @pl.when(step == z.steps - 1)
+
+def layer_scratch(z):
+    return [
+        pltpu.VMEM((10, 8, 128), high),
+        pltpu.VMEM((5, 256, 256), low),
+        pltpu.VMEM((128, 256), low),
+        pltpu.VMEM((z.tile, 128), low),
+        pltpu.VMEM((z.tile_chunks, 128, z.chunk), low),
+        pltpu.VMEM((z.tile // 2, 256), low),
+        pltpu.VMEM((z.tile // 2, 256), low),
+        pltpu.VMEM((z.tile // 2, 256), low),
+        pltpu.VMEM((z.tile // 2, 256), low),
+        pltpu.VMEM((z.tile, 128), high),
+        pltpu.VMEM((z.tile, 128), high),
+        pltpu.VMEM((z.tile // 2, 256), low),
+        pltpu.VMEM((2, z.tile_nodes, 128), low),
+        pltpu.VMEM((2, z.tile_nodes, 128), low),
+        pltpu.VMEM((3, z.tile_nodes, 128), low),
+        pltpu.VMEM((z.tile_nodes, 128), low),
+        pltpu.VMEM((z.tile_nodes, 256), low),
+        pltpu.VMEM((z.tile_slots, 128), low),
+        pltpu.VMEM((z.tile_nodes, 128), low),
+        pltpu.VMEM((z.tile_slots, 128), low),
+        pltpu.VMEM((z.tile_nodes, 128), low),
+    ]
+
+
+def layer_outputs(z, nodes, edges, slots):
+    return [
+        jax.ShapeDtypeStruct((nodes, 128), low),
+        jax.ShapeDtypeStruct((edges, 128), low),
+        jax.ShapeDtypeStruct((nodes, 128), high),
+        jax.ShapeDtypeStruct((edges, 128), high),
+        jax.ShapeDtypeStruct((slots, 128), low),
+    ]
+
+
+def layer_kernel(z, block_ref, *refs):
+    inputs, weights, refs = refs[:8], refs[8:12], refs[12:]
+    grads_in_ref, own, refs = refs[0], refs[1:6], refs[6:]
+    results, grads_ref, staged, refs = refs[:5], refs[5], refs[6:11], refs[11:]
+    own_sem, store_sem, *scratch = refs
+    step = pl.program_id(0)
+    block, steps = block_ref[0], z.tiles - 1
+    slot = lax.rem(step, 2)
+    counts = [result.shape[0] // z.tiles for result in results]
+
+    def stores(at, tile):
+        return [
+            pltpu.make_async_copy(
+                place.at[at], result.at[pl.ds(tile * count, count), :], store_sem.at[at, k]
+            )
+            for k, (place, result, count) in enumerate(zip(staged, results, counts))
+        ]
+
+    own_copies = [
+        pltpu.make_async_copy(
+            place, result.at[pl.ds(block * count, count), :], own_sem.at[k]
+        )
+        for k, (place, result, count) in enumerate(zip(own, results, counts))
+    ]
+
+    @pl.when(step == 0)
     def _():
-        grads_ref[1152:1162, :] = jnp.sum(sums_s[...], axis=1)
-
-
-def layer_call(z, count, slot_ids, recv_ids, edge_in, edge_cot, node_in, node_cot, slot_rows, weights):
+        for copy in own_copies:
+            copy.start()
+        grads_ref[...] = grads_in_ref[...]
+        prepare(weights[0], weights[2], weights[3], *scratch[:3])
+
+    @pl.when(step >= 2)
+    def _():
+        for copy in stores(slot, 0):
+            copy.wait()
+
+    tile = lax.rem(block + 1 + step, z.tiles)
+    places = [place.at[slot] for place in staged]
+    layer_tile(z, tile, *inputs, *weights, *places, grads_ref, *scratch)
+    for copy in stores(slot, tile):
+        copy.start()
+
+    @pl.when(step == steps - 1)
+    def _():
+        close_sums(grads_ref, scratch[0])
+        for copy in own_copies:
+            copy.wait()
+        if steps > 1:
+            for copy in stores(1 - slot, 0):
+                copy.wait()
+        for copy in stores(slot, 0):
+            copy.wait()
+
+
+def layer_call(z, block, inputs, weights, grads, own):
+    steps = z.tiles - 1
+
     def rows_spec(rows):
-        return pl.BlockSpec((rows, 128), lambda i: (i, 0))
+        return pl.BlockSpec((rows, 128), lambda i, block: (lax.rem(block[0] + 1 + i, z.tiles), 0))
 
     def whole(array):
-        return pl.BlockSpec(array.shape, lambda i: (0,) * array.ndim)
-
+        return pl.BlockSpec(array.shape, lambda i, block: (0,) * array.ndim)
+
+    hbm = pl.BlockSpec(memory_space=pltpu.HBM)
+    shapes = layer_outputs(z, z.nodes, z.edges, z.slots)
+    tile_shapes = layer_outputs(z, z.tile_nodes, z.tile, z.tile_slots)
     return pl.pallas_call(
         functools.partial(layer_kernel, z),
-        grid=(z.steps,),
-        in_specs=[
-            pl.BlockSpec(memory_space=pltpu.SMEM),
-            rows_spec(z.tile // 128),
-            rows_spec(z.tile // 128),
-            rows_spec(z.tile),
-            rows_spec(z.tile),
-            rows_spec(z.tile_nodes),
-            rows_spec(z.tile_nodes),
-            rows_spec(z.tile_slots),
-        ]
-        + [whole(w) for w in weights],
-        out_specs=[
-            rows_spec(z.tile_nodes),
-            rows_spec(z.tile),
-            rows_spec(z.tile_nodes),
-            rows_spec(z.tile),
-            rows_spec(z.tile_slots),
-            pl.BlockSpec((z.grad_rows, 128), lambda i: (0, 0)),
-        ],
-        out_shape=[
-            jax.ShapeDtypeStruct((z.nodes, 128), low),
-            jax.ShapeDtypeStruct((z.edges, 128), low),
-            jax.ShapeDtypeStruct((z.nodes, 128), high),
-            jax.ShapeDtypeStruct((z.edges, 128), high),
-            jax.ShapeDtypeStruct((z.slots, 128), low),
-            jax.ShapeDtypeStruct((z.grad_rows, 128), high),
-        ],
-        scratch_shapes=[
-            pltpu.VMEM((z.tile, 128), low),
-            pltpu.VMEM((z.tile_chunks, 128, z.chunk), low),
-            pltpu.VMEM((z.tile // 2, 256), low),
-            pltpu.VMEM((z.tile // 2, 256), low),
-            pltpu.VMEM((z.tile // 2, 256), low),
-            pltpu.VMEM((z.tile // 2, 256), low),
-            pltpu.VMEM((z.tile, 128), high),
-            pltpu.VMEM((z.tile, 128), high),
-            pltpu.VMEM((z.tile // 2, 256), low),
-            pltpu.VMEM((2, z.tile_nodes, 128), low),
-            pltpu.VMEM((2, z.tile_nodes, 128), low),
-            pltpu.VMEM((3, z.tile_nodes, 128), low),
-            pltpu.VMEM((z.tile_nodes, 128), low),
-            pltpu.VMEM((z.tile_nodes, 256), low),
-            pltpu.VMEM((z.tile_slots, 128), low),
-            pltpu.VMEM((z.tile_nodes, 128), low),
-            pltpu.VMEM((z.tile_slots, 128), low),
-            pltpu.VMEM((z.tile_nodes, 128), low),
-            pltpu.VMEM((10, 8, 128), high),
-            pltpu.VMEM((7, 256, 256), low),
-            pltpu.VMEM((128, 256), low),
-        ],
+        grid_spec=pltpu.PrefetchScalarGridSpec(
+            num_scalar_prefetch=1,
+            grid=(steps,),
+            in_specs=[
+                pl.BlockSpec(memory_space=pltpu.SMEM),
+                rows_spec(z.tile // 128),
+                rows_spec(z.tile // 128),
+                rows_spec(z.tile),
+                rows_spec(z.tile),
+                rows_spec(z.tile_nodes),
+                rows_spec(z.tile_nodes),
+                rows_spec(z.tile_slots),
+            ]
+            + [whole(w) for w in weights]
+            + [whole(grads)]
+            + [hbm] * 5,
+            out_specs=[hbm] * 5 + [whole(grads)],
+            scratch_shapes=[pltpu.VMEM((2,) + item.shape, item.dtype) for item in tile_shapes]
+            + [pltpu.SemaphoreType.DMA((5,)), pltpu.SemaphoreType.DMA((2, 5))]
+            + layer_scratch(z),
+        ),
+        out_shape=[*shapes, jax.ShapeDtypeStruct(grads.shape, high)],
         compiler_params=pltpu.CompilerParams(
             dimension_semantics=("arbitrary",), vmem_limit_bytes=VMEM
         ),
         name="layer",
-    )(count, slot_ids, recv_ids, edge_in, edge_cot, node_in, node_cot, slot_rows, *weights)
+    )(block, *inputs, *weights, grads, *own)
 
 
 def signal(semaphore, where):
@@ -543,34 +605,43 @@
     return copy
 
 
-def fetch_kernel(
-    peers,
-    unroll,
-    request_ref,
-    node_ref,
-    rows_ref,
-    asked_ref,
-    wanted_v,
-    asked_v,
-    node_v,
-    node_s,
-    picked_s,
-    out_s,
-    ask_send,
-    ask_recv,
-    row_send,
-    row_recv,
-    load_sem,
-):
+def fetch_kernel(z, peers, unroll, count_ref, *refs):
+    request_ref, sources, weight_refs, refs = refs[0], refs[1:7], refs[7:11], refs[11:]
+    rows_ref, asked_ref, block_ref, results, refs = refs[0], refs[1], refs[2], refs[3:9], refs[9:]
+    wanted_v, asked_v, node_v, node_s, picked_s, out_s, refs = *refs[:6], refs[6:]
+    ask_send, ask_recv, row_send, row_recv, load_sem, store_sem, refs = *refs[:6], refs[6:]
+    loaded, weights, slot_v, staged, scratch = refs[:6], refs[6:10], refs[10], refs[11:17], refs[17:]
     me = lax.axis_index("dom")
     slots = picked_s.shape[0]
+    mates = z.tile_slots // slots
+    blocks = peers // mates
+    block, place = lax.div(me, mates), lax.rem(me, mates)
+
+    def peer(across, along, sign):
+        return (
+            lax.rem(block + (blocks + sign * across), blocks) * mates
+            + lax.rem(place + (mates + sign * along), mates)
+        )
+
+    order = sorted(range(1, blocks), key=lambda across: (abs(2 * across - blocks), across))
+    shifts = [(across, along) for across in order for along in range(mates)]
+    shifts[mates:mates] = [(0, along) for along in range(1, mates)]
     barrier = pltpu.get_barrier_semaphore()
-    for k in range(1, peers):
-        signal(barrier, {"dom": lax.rem(me + k, peers)})
+    for across, along in shifts:
+        signal(barrier, {"dom": peer(across, along, 1)})
     loads = [
         pltpu.make_async_copy(request_ref, wanted_v, load_sem.at[0]),
-        pltpu.make_async_copy(node_ref, node_v, load_sem.at[1]),
+        pltpu.make_async_copy(sources[4], node_v, load_sem.at[1]),
     ]
+    for k, (source, target) in enumerate(zip(sources, loaded)):
+        rows = target.shape[0]
+        loads.append(
+            pltpu.make_async_copy(
+                source.at[pl.ds(block * rows, rows), :], target, load_sem.at[2 + k]
+            )
+        )
+    for k, (source, target) in enumerate(zip(weight_refs, weights)):
+        loads.append(pltpu.make_async_copy(source, target, load_sem.at[8 + k]))
     for load in loads:
         load.start()
     loads[0].wait()
@@ -578,27 +649,34 @@
         asked_v[k] = wanted_v[pl.ds(k, 1), :]
     loads[1].wait()
     node_s[...] = node_v[...].astype(high)
+    block_ref[0] = block
     pl.semaphore_wait(barrier, peers - 1)
-    shifts = [peers // 2 + (k // 2) * (1 - 2 * (k % 2)) for k in range(1, peers)]
-    asks = [
-        send(
-            asked_v.at[lax.rem(me + k, peers)],
-            asked_v.at[peers + me],
-            ask_send.at[k],
-            ask_recv.at[k],
-            {"dom": lax.rem(me + k, peers)},
+    asks = []
+    for across, along in shifts:
+        other, k = peer(across, along, 1), across * mates + along
+        asks.append(
+            send(
+                asked_v.at[other],
+                asked_v.at[peers + me],
+                ask_send.at[k],
+                ask_recv.at[k],
+                {"dom": other},
+            )
         )
-        for k in shifts
-    ]
     asked_v[peers + me] = asked_v[me]
+    grads_v = staged[5]
+    grads_v[...] = jnp.zeros_like(grads_v)
+    for load in loads[8:]:
+        load.wait()
+    prepare(weights[0], weights[2], weights[3], *scratch[:3])
     for ask in asks:
         ask.wait_recv()
     local = pltpu.make_async_copy(asked_v.at[pl.ds(peers, peers)], asked_ref, load_sem.at[0])
     local.start()
     local.wait()
-    sends = []
-    for k in shifts + [0]:
-        other = lax.rem(me + (peers - k), peers)
+    sends, arrivals = [], []
+    for across, along in shifts + [(0, 0)]:
+        other, k = peer(across, along, -1), across * mates + along
 
         @pl.loop(0, slots // unroll)
         def _(group):
@@ -609,54 +687,91 @@
 
         out_s[other] = picked_s[...].astype(low)
         if k:
-            sends.append(
-                send(
-                    out_s.at[other],
-                    rows_ref.at[me],
-                    row_send.at[k],
-                    row_recv.at[k],
-                    {"dom": other},
-                )
+            copy = send(
+                out_s.at[other],
+                rows_ref.at[me],
+                row_send.at[k],
+                row_recv.at[k],
+                {"dom": other},
             )
+            (sends if across else arrivals).append(copy)
     local = pltpu.make_async_copy(out_s.at[me], rows_ref.at[me], load_sem.at[0])
     local.start()
+    local.wait()
+    for copy in arrivals:
+        copy.wait()
+    local = pltpu.make_async_copy(
+        rows_ref.at[pl.ds(block * mates, mates)], slot_v, load_sem.at[0]
+    )
+    local.start()
+    for load in loads[2:8]:
+        load.wait()
+    local.wait()
+    slot_rows = slot_v.reshape(mates * slots, 128)
+    layer_tile(z, block, count_ref, *loaded, slot_rows, *weights, *staged, *scratch)
+    close_sums(grads_v, scratch[0])
+    stores = [
+        pltpu.make_async_copy(place, result, store_sem.at[k])
+        for k, (place, result) in enumerate(zip(staged, results))
+    ]
+    for store in stores:
+        store.start()
     for copy in asks:
         copy.wait_send()
-    local.wait()
     for copy in sends:
         copy.wait()
-
-
-def fetch_call(peers, request, node_in):
+    for store in stores:
+        store.wait()
+
+
+def fetch_call(z, peers, count, request, ids, edges, nodes, weights):
     slots = request.shape[2]
+    mates = z.tile_slots // slots
     dma = pltpu.SemaphoreType.DMA
     hbm = pl.BlockSpec(memory_space=pltpu.HBM)
+    smem = pl.BlockSpec(memory_space=pltpu.SMEM)
+    tile_shapes = layer_outputs(z, z.tile_nodes, z.tile, z.tile_slots)
+    tile_shapes.append(jax.ShapeDtypeStruct((z.grad_rows, 128), high))
+    ids_rows = z.tile // 128
     return pl.pallas_call(
-        functools.partial(fetch_kernel, peers, 32),
-        in_specs=[hbm, hbm],
-        out_specs=[hbm, pl.BlockSpec(memory_space=pltpu.SMEM)],
+        functools.partial(fetch_kernel, z, peers, 32),
+        in_specs=[smem] + [hbm] * 11,
+        out_specs=[hbm, smem, smem] + [hbm] * 6,
         out_shape=[
             jax.ShapeDtypeStruct((peers, slots, 128), low),
             jax.ShapeDtypeStruct((peers, 1, slots), jnp.int32),
+            jax.ShapeDtypeStruct((1,), jnp.int32),
+            *tile_shapes,
         ],
         scratch_shapes=[
             pltpu.VMEM((peers, slots), jnp.int32),
             pltpu.VMEM((2 * peers, 1, slots), jnp.int32),
-            pltpu.VMEM(node_in.shape, low),
-            pltpu.VMEM(node_in.shape, high),
+            pltpu.VMEM((z.nodes, 128), low),
+            pltpu.VMEM((z.nodes, 128), high),
             pltpu.VMEM((slots, 128), high),
             pltpu.VMEM((peers, slots, 128), low),
             dma((peers,)),
             dma((peers,)),
             dma((peers,)),
             dma((peers,)),
-            dma((2,)),
+            dma((12,)),
+            dma((6,)),
+            pltpu.VMEM((ids_rows, 128), jnp.int32),
+            pltpu.VMEM((ids_rows, 128), jnp.int32),
+            pltpu.VMEM((z.tile, 128), low),
+            pltpu.VMEM((z.tile, 128), low),
+            pltpu.VMEM((z.tile_nodes, 128), low),
+            pltpu.VMEM((z.tile_nodes, 128), low),
+            *[pltpu.VMEM(w.shape, w.dtype) for w in weights],
+            pltpu.VMEM((mates, slots, 128), low),
+            *[pltpu.VMEM(item.shape, item.dtype) for item in tile_shapes],
+            *layer_scratch(z),
         ],
         compiler_params=pltpu.CompilerParams(
             collective_id=0, has_side_effects=True, vmem_limit_bytes=VMEM
         ),
         name="fetch",
-    )(request.reshape(peers, slots), node_in)
+    )(count, request.reshape(peers, slots), *ids, *edges, *nodes, *weights)
 
 
 def reduce_kernel(
@@ -961,18 +1076,33 @@
     groups, peers = lax.axis_size("grp"), lax.axis_size("dom")
     slots = request.shape[2]
     z = Sizes(edge_in.shape[0], node_in.shape[0], peers * slots, groups * peers)
-    slot_rows, asked = fetch_call(peers, request, node_in)
+    weights = tensors[::4]
+    ids = (edge_slot.reshape(-1, 128), edge_receiver.reshape(-1, 128))
+    slot_rows, asked, block, *own, grads = fetch_call(
+        z,
+        peers,
+        edge_count,
+        request,
+        ids,
+        (edge_in, edge_cot),
+        (node_in, node_cot),
+        weights,
+    )
     node_out, edge_out, node_part, edge_grad, slot_grad, grads = layer_call(
         z,
-        edge_count,
-        edge_slot.reshape(-1, 128),
-        edge_receiver.reshape(-1, 128),
-        edge_in,
-        edge_cot,
-        node_in,
-        node_cot,
-        slot_rows.reshape(peers * slots, 128),
-        tensors[::4],
+        block,
+        (
+            edge_count,
+            *ids,
+            edge_in,
+            edge_cot,
+            node_in,
+            node_cot,
+            slot_rows.reshape(peers * slots, 128),
+        ),
+        weights,
+        grads,
+        own,
     )
     summed, returned = reduce_call(groups, peers, grads, slot_grad.reshape(peers, slots, 128))
     flat = [tensor.reshape(-1, 128) for tensor in tensors]

time: 137 us -> 292 us (2.13)
  Pallas kernels: 135 us -> 291 us
    pallas_call x2, Pallas kernels: 100 us -> 256 us  [the longest x1 224 us: layer_call(): pl.pallas_call(functools.partial(layer_kernel, z), grid_spec=pltpu.Prefet...]
where the time goes in v4:
time: 292 us
  Pallas kernels  291 us (100%)
    pallas_call x1, Pallas kernels, layer_call(): pl.pallas_call(functools.partial(layer_kernel, z), grid_spec=pltpu.Prefet...  224 us
    pallas_call x1, Pallas kernels, fetch_call(): pl.pallas_call(functools.partial(fetch_kernel, z, peers, 32), in_specs=[s...  31.7 us
    pallas_call x1, Pallas kernels, reduce_call(): pl.pallas_call(functools.partial(reduce_kernel, groups, peers), in_specs=...  22.6 us
    pallas_call x1, Pallas kernels, finish_call(): pl.pallas_call(functools.partial(finish_kernel, 32), in_specs=[smem] + [h...  12.2 us

profile of v4, /device:TPU:0, one launch (start us, length us, event | category | flops | bytes accessed | tf_op | source)
XLA Modules:
  0.0 292.2 jit_solution(2679634659935424948)
XLA Ops:
  1.3 31.7 %fetch.1 = (bf16[8,256,128]{2,1,0:T(8,128)(2,1)}, s32[8,1,256]{2,1,0:T(1,128)}, s32[1]{0:T(128)}, bf16[1024,128]{1,0:T(8,128)(2,1)}, bf16[8192,128]{1,0:T(8,128)...) custom-call(s32[1]{0:T(128)S(6)} %copy.49.count_ref.refs_0_, ...), custom_call_target="tpu_custom_call" | custom-call | tf_op jit(solution)/shard_map/fetch/pallas_call | solution.py:736
  33.0 224.2 %layer.1 = (bf16[4096,128]{1,0:T(8,128)(2,1)}, bf16[32768,128]{1,0:T(8,128)(2,1)}, f32[4096,128]{1,0:T(8,128)}, f32[32768,128]{1,0:T(8,128)}, bf16[2048,128]{1,0:T(8,128)(2,1)}, /*index=5*/f32[1536,128]{1,0:T(8,128)}) custom-call(s32[1]{0:T(128)} %get-tuple-element.64.block_ref, s32[1]{0:T(128)S(6)} %copy.49.count_ref.refs_0_, s32[256,128]{1,0:T(8,128)} %bitcast.18, ...), custom_call_target="tpu_custom_call" | custom-call | tf_op jit(solution)/shard_map/layer/pallas_call | solution.py:560
  257.2 22.6 %reduce.1 = (bf16[1536,128]{1,0:T(8,128)(2,1)}, bf16[8,256,128]{2,1,0:T(8,128)(2,1)}) custom-call(f32[1536,128]{1,0:T(8,128)} %get-tuple-element.75.grads_ref, bf16[8,256,128]{2,1,0:T(8,128)(2,1)} %bitcast.22), custom_call_target="tpu_custom_call" | custom-call | tf_op jit(solution)/shard_map/reduce/pallas_call | solution.py:928
  279.9 12.2 %finish.1 = (f32[1]{0:T(128)}, f32[384,128]{1,0:T(8,128)}, f32[384,128]{1,0:T(8,128)}, f32[384,128]{1,0:T(8,128)}, bf16[384,128]{1,0:T(8,128)(2,1)}, /*index=5*/...) custom-call(s32[8,1,256]{2,1,0:T(1,128)} %get-tuple-element.74.asked, ...), custom_call_target="tpu_custom_call" | custom-call | tf_op jit(solution)/shard_map/finish/pallas_call | solution.py:1044

commit v5 on v4

--- a/solution.py
+++ b/solution.py
@@ -28,7 +28,7 @@
 GAP = 2
 PIECE = 64
 PIECE_NORM = 32
-VMEM = 60 * 1024 * 1024
+VMEM = 62 * 1024 * 1024
 PAIRS = 8
 
 
@@ -50,11 +50,11 @@
 
 def gelu_pair(x):
     square = x * x
-    u = x * (gelu_in + gelu_cube * square)
-    s = 0.5 + 0.5 * jnp.tanh(u)
-    value = x * s
-    slope = s + (value - value * s) * (2.0 * gelu_in + (6.0 * gelu_cube) * square)
-    return value, slope
+    t = jnp.tanh(x * (gelu_in + gelu_cube * square))
+    above = 1.0 + t
+    value = (0.5 * x) * above
+    slope = 0.5 * above + (value * (1.0 - t)) * (gelu_in + (3.0 * gelu_cube) * square)
+    return value.astype(low), slope.astype(low)
 
 
 def fold_rows(values):
@@ -193,8 +193,6 @@
     table_s,
     slot_pre_s,
     node_pre_s,
-    slot_sum_s,
-    recv_sum_s,
 ):
     chunk, cn, cs = z.chunk, z.chunk_nodes, z.chunk_slots
     pad = 128 - cn - cs
@@ -252,7 +250,7 @@
             for k in range(z.sub):
                 block = index * z.sub + k
                 hot_t = hot_block(block, k)
-                pick_t[index, :, k * 128 : (k + 1) * 128] = hot_t
+                pick_t[index, :, k * 128 : (k + 1) * 128] = hot_t[: cs + cn]
                 pick_s[pl.ds(block * 128, 128), :] = hot_t.T
         yield
         pres = []
@@ -291,7 +289,7 @@
                 inverse = jnp.where(live, inverse, 0.0)
                 normed = center * inverse
                 normed_s[rows, :] = normed
-                inverse_s[rows, :] = inverse
+                inverse_s[rows, :] = inverse.astype(low)
                 message = jnp.where(live, normed * vec[3] + vec[4], 0.0)
                 edge_out_ref[rows, :] = (edge_in_ref[rows, :].astype(high) + message).astype(low)
                 message_s[
@@ -316,14 +314,14 @@
         pre = dot(entry, node_low)
         yield
         for first, last in parts:
-            act, slope = gelu_pair((pre[first:last] + vec[5]).astype(low))
+            act, slope = gelu_pair(pre[first:last] + vec[5])
             node_act_s[0, here(first, last), :] = act
             node_slope_s[0, here(first, last), :] = slope
         yield
         pre = dot(node_act_s[0, rows, :], inner_low[2])
         yield
         for first, last in parts:
-            act, slope = gelu_pair((pre[first:last] + vec[6]).astype(low))
+            act, slope = gelu_pair(pre[first:last] + vec[6])
             node_act_s[1, here(first, last), :] = act
             node_slope_s[1, here(first, last), :] = slope
         yield
@@ -346,18 +344,19 @@
             mean_cross = jnp.mean(upper * normed, axis=1, keepdims=True)
             d_three = inverse * (upper - mean_plain - normed * mean_cross)
             sums_s[7] += fold_rows(d_three)
-            node_back_s[2, piece, :] = d_three.astype(low)
+            node_back_s[piece, :] = d_three.astype(low)
         yield
         for k in (1, 0):
-            back = dot_nt(node_back_s[k + 1, rows, :], inner_low[2 + k])
+            upper = node_back_s[rows, :] if k else node_slope_s[1, rows, :]
+            back = dot_nt(upper, inner_low[2 + k])
             yield
             for first, last in parts:
                 piece = here(first, last)
                 value = back[first:last] * node_slope_s[k, piece, :].astype(high)
                 sums_s[5 + k] += fold_rows(value)
-                node_back_s[k, piece, :] = value.astype(low)
+                node_slope_s[k, piece, :] = value.astype(low)
             yield
-        back = dot_nt(node_back_s[0, rows, :], node_low)
+        back = dot_nt(node_slope_s[0, rows, :], node_low)
         for first, last in parts:
             piece = here(first, last)
             node_grad_ref[piece, :] = node_cot_ref[piece, :].astype(high) + back[first:last, :128]
@@ -365,9 +364,9 @@
         yield
         table_s[rows, 128:] = dot(table_s[rows, :128], gain_part).astype(low)
         yield
-        grads_ref[384:640, :] += dot_tn(entry, node_back_s[0, rows, :])
-        grads_ref[896:1024, :] += dot_tn(node_act_s[0, rows, :], node_back_s[1, rows, :])
-        grads_ref[1024:1152, :] += dot_tn(node_act_s[1, rows, :], node_back_s[2, rows, :])
+        grads_ref[384:640, :] += dot_tn(entry, node_slope_s[0, rows, :])
+        grads_ref[896:1024, :] += dot_tn(node_act_s[0, rows, :], node_slope_s[1, rows, :])
+        grads_ref[1024:1152, :] += dot_tn(node_act_s[1, rows, :], node_back_s[rows, :])
         yield
 
     def edge_backward(pair):
@@ -428,10 +427,10 @@
         second = total[256 + cs + cn :, 128:]
         node_rows = pl.ds(pair * z.pair_nodes, z.pair_nodes)
         slot_rows = pl.ds(pair * z.pair_slots, z.pair_slots)
-        slot_sum_s[slot_rows, :] = jnp.concatenate([first[:cs], second[:cs]], axis=0).astype(low)
+        slot_pre_s[slot_rows, :] = jnp.concatenate([first[:cs], second[:cs]], axis=0).astype(low)
         recv_sum = jnp.concatenate([first[cs:], second[cs:]], axis=0)
         sums_s[0] += fold_rows(recv_sum)
-        recv_sum_s[node_rows, :] = recv_sum.astype(low)
+        node_pre_s[node_rows, :] = recv_sum.astype(low)
         yield
         for k, act_s, gradient_s in ((1, act_one_s, slope_two_s), (2, act_two_s, message_s)):
             total = dot(
@@ -444,11 +443,11 @@
     def group_end(group):
         node_rows = pl.ds(group * z.group_nodes, z.group_nodes)
         slot_rows = pl.ds(group * z.group_slots, z.group_slots)
-        slot_grad_ref[slot_rows, :] = dot_nt(slot_sum_s[slot_rows, :], w_slot).astype(low)
-        node_grad_ref[node_rows, :] += dot_nt(recv_sum_s[node_rows, :], w_recv)
-        yield
-        grads_ref[128:256, :] += dot_tn(slot_ref[slot_rows, :], slot_sum_s[slot_rows, :])
-        grads_ref[256:384, :] += dot_tn(node_in_ref[node_rows, :], recv_sum_s[node_rows, :])
+        slot_grad_ref[slot_rows, :] = dot_nt(slot_pre_s[slot_rows, :], w_slot).astype(low)
+        node_grad_ref[node_rows, :] += dot_nt(node_pre_s[node_rows, :], w_recv)
+        yield
+        grads_ref[128:256, :] += dot_tn(slot_ref[slot_rows, :], slot_pre_s[slot_rows, :])
+        grads_ref[256:384, :] += dot_tn(node_in_ref[node_rows, :], node_pre_s[node_rows, :])
         yield
 
     emit(z.pairs, z.per_group, edge_forward, node_phase, edge_backward, group_end)
@@ -460,21 +459,19 @@
         pltpu.VMEM((5, 256, 256), low),
         pltpu.VMEM((128, 256), low),
         pltpu.VMEM((z.tile, 128), low),
-        pltpu.VMEM((z.tile_chunks, 128, z.chunk), low),
+        pltpu.VMEM((z.tile_chunks, z.chunk_slots + z.chunk_nodes, z.chunk), low),
         pltpu.VMEM((z.tile // 2, 256), low),
         pltpu.VMEM((z.tile // 2, 256), low),
         pltpu.VMEM((z.tile // 2, 256), low),
         pltpu.VMEM((z.tile // 2, 256), low),
         pltpu.VMEM((z.tile, 128), high),
-        pltpu.VMEM((z.tile, 128), high),
+        pltpu.VMEM((z.tile, 128), low),
         pltpu.VMEM((z.tile // 2, 256), low),
         pltpu.VMEM((2, z.tile_nodes, 128), low),
         pltpu.VMEM((2, z.tile_nodes, 128), low),
-        pltpu.VMEM((3, z.tile_nodes, 128), low),
+        pltpu.VMEM((z.tile_nodes, 128), low),
         pltpu.VMEM((z.tile_nodes, 128), low),
         pltpu.VMEM((z.tile_nodes, 256), low),
-        pltpu.VMEM((z.tile_slots, 128), low),
-        pltpu.VMEM((z.tile_nodes, 128), low),
         pltpu.VMEM((z.tile_slots, 128), low),
         pltpu.VMEM((z.tile_nodes, 128), low),
     ]
@@ -494,7 +491,7 @@
     inputs, weights, refs = refs[:8], refs[8:12], refs[12:]
     grads_in_ref, own, refs = refs[0], refs[1:6], refs[6:]
     results, grads_ref, staged, refs = refs[:5], refs[5], refs[6:11], refs[11:]
-    own_sem, store_sem, *scratch = refs
+    carried, (own_sem, store_sem, *scratch) = refs[:5], refs[5:]
     step = pl.program_id(0)
     block, steps = block_ref[0], z.tiles - 1
     slot = lax.rem(step, 2)
@@ -508,19 +505,32 @@
             for k, (place, result, count) in enumerate(zip(staged, results, counts))
         ]
 
-    own_copies = [
+    own_loads = [
+        pltpu.make_async_copy(source, place, own_sem.at[0, k])
+        for k, (source, place) in enumerate(zip(own, carried))
+    ]
+    own_stores = [
         pltpu.make_async_copy(
-            place, result.at[pl.ds(block * count, count), :], own_sem.at[k]
+            place, result.at[pl.ds(block * count, count), :], own_sem.at[1, k]
         )
-        for k, (place, result, count) in enumerate(zip(own, results, counts))
+        for k, (place, result, count) in enumerate(zip(carried, results, counts))
     ]
+
+    def pass_on():
+        for load, store in zip(own_loads, own_stores):
+            load.wait()
+            store.start()
 
     @pl.when(step == 0)
     def _():
-        for copy in own_copies:
-            copy.start()
+        for load in own_loads:
+            load.start()
         grads_ref[...] = grads_in_ref[...]
         prepare(weights[0], weights[2], weights[3], *scratch[:3])
+
+    @pl.when(step == 1)
+    def _():
+        pass_on()
 
     @pl.when(step >= 2)
     def _():
@@ -536,8 +546,10 @@
     @pl.when(step == steps - 1)
     def _():
         close_sums(grads_ref, scratch[0])
-        for copy in own_copies:
-            copy.wait()
+        if steps == 1:
+            pass_on()
+        for store in own_stores:
+            store.wait()
         if steps > 1:
             for copy in stores(1 - slot, 0):
                 copy.wait()
@@ -552,7 +564,9 @@
         return pl.BlockSpec((rows, 128), lambda i, block: (lax.rem(block[0] + 1 + i, z.tiles), 0))
 
     def whole(array):
-        return pl.BlockSpec(array.shape, lambda i, block: (0,) * array.ndim)
+        return pl.BlockSpec(
+            array.shape, lambda i, block: (0,) * array.ndim, pipeline_mode=pl.Buffered(1)
+        )
 
     hbm = pl.BlockSpec(memory_space=pltpu.HBM)
     shapes = layer_outputs(z, z.nodes, z.edges, z.slots)
@@ -575,9 +589,10 @@
             + [whole(w) for w in weights]
             + [whole(grads)]
             + [hbm] * 5,
-            out_specs=[hbm] * 5 + [whole(grads)],
+            out_specs=[hbm] * 5 + [pl.BlockSpec(grads.shape, lambda i, block: (0, 0))],
             scratch_shapes=[pltpu.VMEM((2,) + item.shape, item.dtype) for item in tile_shapes]
-            + [pltpu.SemaphoreType.DMA((5,)), pltpu.SemaphoreType.DMA((2, 5))]
+            + [pltpu.VMEM(item.shape, item.dtype) for item in tile_shapes]
+            + [pltpu.SemaphoreType.DMA((2, 5)), pltpu.SemaphoreType.DMA((2, 5))]
             + layer_scratch(z),
         ),
         out_shape=[*shapes, jax.ShapeDtypeStruct(grads.shape, high)],
@@ -685,28 +700,17 @@
                 index = asked_ref[other, 0, row]
                 picked_s[pl.ds(row, 1), :] = node_s[pl.ds(index, 1), :]
 
+        if not k:
+            slot_v[place] = picked_s[...].astype(low)
+            continue
         out_s[other] = picked_s[...].astype(low)
-        if k:
-            copy = send(
-                out_s.at[other],
-                rows_ref.at[me],
-                row_send.at[k],
-                row_recv.at[k],
-                {"dom": other},
-            )
-            (sends if across else arrivals).append(copy)
-    local = pltpu.make_async_copy(out_s.at[me], rows_ref.at[me], load_sem.at[0])
-    local.start()
-    local.wait()
+        target = rows_ref.at[me] if across else slot_v.at[place]
+        copy = send(out_s.at[other], target, row_send.at[k], row_recv.at[k], {"dom": other})
+        (sends if across else arrivals).append(copy)
+    for load in loads[2:8]:
+        load.wait()
     for copy in arrivals:
         copy.wait()
-    local = pltpu.make_async_copy(
-        rows_ref.at[pl.ds(block * mates, mates)], slot_v, load_sem.at[0]
-    )
-    local.start()
-    for load in loads[2:8]:
-        load.wait()
-    local.wait()
     slot_rows = slot_v.reshape(mates * slots, 128)
     layer_tile(z, block, count_ref, *loaded, slot_rows, *weights, *staged, *scratch)
     close_sums(grads_v, scratch[0])

time: 292 us -> 116 us (0.40)
  Pallas kernels: 291 us -> 114 us
    pallas_call x1, Pallas kernels: 224 us -> 48.5 us  [layer_call(): pl.pallas_call(functools.partial(layer_kernel, z), grid_spec=pltpu.Prefet...]
where the time goes in v5:
time: 116 us
  Pallas kernels  114 us (98%)
  between operations  1.5 us (1%)
    pallas_call x1, Pallas kernels, layer_call(): pl.pallas_call(functools.partial(layer_kernel, z), grid_spec=pltpu.Prefet...  48.5 us
    pallas_call x1, Pallas kernels, fetch_call(): pl.pallas_call(functools.partial(fetch_kernel, z, peers, 32), in_specs=[s...  30.8 us
    pallas_call x1, Pallas kernels, reduce_call(): pl.pallas_call(functools.partial(reduce_kernel, groups, peers), in_specs=...  22.6 us
    pallas_call x1, Pallas kernels, finish_call(): pl.pallas_call(functools.partial(finish_kernel, 32), in_specs=[smem] + [h...  12.2 us

profile of v5, /device:TPU:0, one launch (start us, length us, event | category | flops | bytes accessed | tf_op | source)
XLA Modules:
  0.0 115.6 jit_solution(331345404835652850)
XLA Ops:
  1.3 30.8 %fetch.1 = (bf16[8,256,128]{2,1,0:T(8,128)(2,1)}, s32[8,1,256]{2,1,0:T(1,128)}, s32[1]{0:T(128)}, bf16[1024,128]{1,0:T(8,128)(2,1)}, bf16[8192,128]{1,0:T(8,128)...) custom-call(s32[1]{0:T(128)S(6)} %copy.49.count_ref.refs_0_, ...), custom_call_target="tpu_custom_call" | custom-call | tf_op jit(solution)/shard_map/fetch/pallas_call | solution.py:740
  32.1 48.5 %layer.1 = (bf16[4096,128]{1,0:T(8,128)(2,1)}, bf16[32768,128]{1,0:T(8,128)(2,1)}, f32[4096,128]{1,0:T(8,128)}, f32[32768,128]{1,0:T(8,128)}, bf16[2048,128]{1,0:T(8,128)(2,1)}, /*index=5*/f32[1536,128]{1,0:T(8,128)}) custom-call(s32[1]{0:T(128)} %get-tuple-element.64.block_ref, s32[1]{0:T(128)S(6)} %copy.49.count_ref.refs_0_, s32[256,128]{1,0:T(8,128)} %bitcast.18, ...), custom_call_target="tpu_custom_call" | custom-call | tf_op jit(solution)/shard_map/layer/pallas_call | solution.py:574
  80.6 22.6 %reduce.1 = (bf16[1536,128]{1,0:T(8,128)(2,1)}, bf16[8,256,128]{2,1,0:T(8,128)(2,1)}) custom-call(f32[1536,128]{1,0:T(8,128)} %get-tuple-element.75.grads_ref, bf16[8,256,128]{2,1,0:T(8,128)(2,1)} %bitcast.22), custom_call_target="tpu_custom_call" | custom-call | tf_op jit(solution)/shard_map/reduce/pallas_call | solution.py:932
  103.3 12.2 %finish.1 = (f32[1]{0:T(128)}, f32[384,128]{1,0:T(8,128)}, f32[384,128]{1,0:T(8,128)}, f32[384,128]{1,0:T(8,128)}, bf16[384,128]{1,0:T(8,128)(2,1)}, /*index=5*/...) custom-call(s32[8,1,256]{2,1,0:T(1,128)} %get-tuple-element.74.asked, ...), custom_call_target="tpu_custom_call" | custom-call | tf_op jit(solution)/shard_map/finish/pallas_call | solution.py:1048

commit v6 on v3

--- a/solution.py
+++ b/solution.py
@@ -25,11 +25,11 @@
 low = jnp.bfloat16
 high = jnp.float32
 
-GAP = 2
+GAP = 4
 PIECE = 64
 PIECE_NORM = 32
 VMEM = 60 * 1024 * 1024
-PAIRS = 2
+PAIRS = 8
 
 
 def dot(operand, weights):
@@ -50,11 +50,11 @@
 
 def gelu_pair(x):
     square = x * x
-    u = x * (gelu_in + gelu_cube * square)
-    s = 0.5 + 0.5 * jnp.tanh(u)
-    value = x * s
-    slope = s + (value - value * s) * (2.0 * gelu_in + (6.0 * gelu_cube) * square)
-    return value, slope
+    t = jnp.tanh(x * (gelu_in + gelu_cube * square))
+    above = 1.0 + t
+    value = (0.5 * x) * above
+    slope = 0.5 * above + (value * (1.0 - t)) * (gelu_in + (3.0 * gelu_cube) * square)
+    return value.astype(low), slope.astype(low)
 
 
 def fold_rows(values):
@@ -104,8 +104,8 @@
         self.chunk_slots = self.sub * self.swin
         self.chunk_nodes = self.sub * self.rwin
         self.pair_nodes, self.pair_slots = 2 * self.chunk_nodes, 2 * self.chunk_slots
-        self.per_group = 2
-        self.pairs = max(PAIRS, 1024 // (2 * self.chunk))
+        self.per_group = 4
+        self.pairs = PAIRS
         self.group_nodes = self.per_group * self.pair_nodes
         self.group_slots = self.per_group * self.pair_slots
         self.tile = self.pairs * 2 * self.chunk
@@ -253,7 +253,7 @@
             for k in range(z.sub):
                 block = index * z.sub + k
                 hot_t = hot_block(block, k)
-                pick_t[index, :, k * 128 : (k + 1) * 128] = hot_t
+                pick_t[index, :, k * 128 : (k + 1) * 128] = hot_t[: cs + cn]
                 pick_s[pl.ds(block * 128, 128), :] = hot_t.T
         yield
         pres = []
@@ -317,14 +317,14 @@
         pre = dot(entry, node_low)
         yield
         for first, last in parts:
-            act, slope = gelu_pair((pre[first:last] + vec[5]).astype(low))
+            act, slope = gelu_pair(pre[first:last] + vec[5])
             node_act_s[0, here(first, last), :] = act
             node_slope_s[0, here(first, last), :] = slope
         yield
         pre = dot(node_act_s[0, rows, :], inner_low[2])
         yield
         for first, last in parts:
-            act, slope = gelu_pair((pre[first:last] + vec[6]).astype(low))
+            act, slope = gelu_pair(pre[first:last] + vec[6])
             node_act_s[1, here(first, last), :] = act
             node_slope_s[1, here(first, last), :] = slope
         yield
@@ -498,7 +498,7 @@
         ],
         scratch_shapes=[
             pltpu.VMEM((z.tile, 128), low),
-            pltpu.VMEM((z.tile_chunks, 128, z.chunk), low),
+            pltpu.VMEM((z.tile_chunks, z.chunk_slots + z.chunk_nodes, z.chunk), low),
             pltpu.VMEM((z.tile // 2, 256), low),
             pltpu.VMEM((z.tile // 2, 256), low),
             pltpu.VMEM((z.tile // 2, 256), low),

time: 137 us -> 118 us (0.86)
  Pallas kernels: 135 us -> 117 us
    pallas_call x1, Pallas kernels: 78.3 us -> 59.7 us  [layer_call(): pl.pallas_call(functools.partial(layer_kernel, z), grid=(z.steps,), in_sp...]
where the time goes in v6:
time: 118 us
  Pallas kernels  117 us (99%)
  between operations  1.34 us (1%)
    pallas_call x1, Pallas kernels, layer_call(): pl.pallas_call(functools.partial(layer_kernel, z), grid=(z.steps,), in_sp...  59.7 us
    pallas_call x1, Pallas kernels, reduce_call(): pl.pallas_call(functools.partial(reduce_kernel, groups, peers), in_specs=...  23.1 us
    pallas_call x1, Pallas kernels, fetch_call(): pl.pallas_call(functools.partial(fetch_kernel, peers, 32), in_specs=[hbm,...  21.7 us
    pallas_call x1, Pallas kernels, finish_call(): pl.pallas_call(functools.partial(finish_kernel, 32), in_specs=[smem] + [h...  12.2 us

profile of v6, /device:TPU:0, one launch (start us, length us, event | category | flops | bytes accessed | tf_op | source)
XLA Modules:
  0.0 118.0 jit_solution(7536143449547875919)
XLA Ops:
  1.3 21.7 %fetch.1 = (bf16[8,256,128]{2,1,0:T(8,128)(2,1)}, s32[8,1,256]{2,1,0:T(1,128)}) custom-call(s32[8,256]{1,0:T(8,128)} %bitcast.25, bf16[4096,128]{1,0:T(8,128)(2,1)} %node_in_ref.1), custom_call_target="tpu_custom_call" | custom-call | tf_op jit(solution)/shard_map/fetch/pallas_call | solution.py:634
  23.0 59.7 %layer.1 = (bf16[4096,128]{1,0:T(8,128)(2,1)}, bf16[32768,128]{1,0:T(8,128)(2,1)}, f32[4096,128]{1,0:T(8,128)}, f32[32768,128]{1,0:T(8,128)}, bf16[2048,128]{1,0:T(8,128)(2,1)}, /*index=5*/f32[1536,128]{1,0:T(8,128)}) custom-call(s32[1]{0:T(128)S(6)} %copy.49.count_ref, s32[256,128]{1,0:T(8,128)} %bitcast.23, s32[256,128]{1,0:T(8,128)} %bitcast.24, ...), custom_call_target="tpu_custom_call" | custom-call | tf_op jit(solution)/shard_map/layer/pallas_call | solution.py:469
  82.7 23.1 %reduce.1 = (bf16[1536,128]{1,0:T(8,128)(2,1)}, bf16[8,256,128]{2,1,0:T(8,128)(2,1)}) custom-call(f32[1536,128]{1,0:T(8,128)} %get-tuple-element.61.grads_ref, bf16[8,256,128]{2,1,0:T(8,128)(2,1)} %bitcast.18), custom_call_target="tpu_custom_call" | custom-call | tf_op jit(solution)/shard_map/reduce/pallas_call | solution.py:813
  105.9 12.2 %finish.1 = (f32[1]{0:T(128)}, f32[384,128]{1,0:T(8,128)}, f32[384,128]{1,0:T(8,128)}, f32[384,128]{1,0:T(8,128)}, bf16[384,128]{1,0:T(8,128)(2,1)}, /*index=5*/...) custom-call(s32[8,1,256]{2,1,0:T(1,128)} %get-tuple-element.60.asked, ...), custom_call_target="tpu_custom_call" | custom-call | tf_op jit(solution)/shard_map/finish/pallas_call | solution.py:929
